TPU v7x, 512 devices: a whole 4x8x8 slice. The times are simulated.
512 devices in a mesh: dp: 128 (over z_lo, x, y, core), tensor: 4 (over z_hi).
Axes of the slice: x: 4, y: 8, z: 8 (z_hi: 4, z_lo: 2; z = z_hi * 2 + z_lo), core: 2. Of those that a mesh axis runs over, the one named last changes fastest.
Arguments:
- hidden_states: bfloat16 [16384, 5376], P('dp', 'tensor'), may hold values from -2 to 2
- embedding: bfloat16 [4096, 5376], P(('dp', 'tensor')), may hold values from -6 to 6
- targets: int32 [16384], P('dp'), may hold values from 0 to 4095
- prior_lse: float32 [16384], P('dp'), may hold values from 9 to 15
Outputs:
- loss: float32 [16384], P('dp')
- hidden_grad: bfloat16 [16384, 5376], P('dp', 'tensor')
All inputs are finite; a program needn't handle non-finite values.
Results may differ from a plain program's by a relative error of at most 0.012.
Values may be sent and summed in bfloat16 or wider, within the bound.
A program may use at most 64 MiB of HBM per device.

v0:
```python
import jax
import jax.numpy as jnp
from jax import lax
from jax.sharding import PartitionSpec as P


def body(hidden_states, embedding, targets, prior_lse):
    hidden = lax.all_gather(hidden_states, "tensor", axis=1, tiled=True)
    tp_rank = lax.axis_index("tensor")
    n_parts = lax.axis_size("tensor")
    row_count = embedding.shape[0]
    block_id = targets // row_count
    owner = block_id % n_parts
    column = block_id // n_parts * row_count + targets % row_count
    column = jnp.where(owner == tp_rank, column, -1)
    gathered = lax.all_gather(embedding, "dp", axis=0, tiled=True)
    logits = jnp.einsum("td,vd->tv", hidden, gathered, preferred_element_type=jnp.float32)
    col_index = jnp.arange(logits.shape[1], dtype=jnp.int32)
    row_peak = jnp.max(logits, axis=1)
    row_total = jnp.sum(jnp.exp(logits - row_peak[:, None]), axis=1)
    row_target = jnp.sum(jnp.where(col_index[None, :] == column[:, None], logits, 0.0), axis=1)
    all_peak = lax.pmax(row_peak, "tensor")
    all_total, all_target = lax.psum(
        (row_total * jnp.exp(row_peak - all_peak), row_target), "tensor"
    )
    top_value = jnp.maximum(all_peak, prior_lse)
    lse = top_value + jnp.log(
        all_total * jnp.exp(all_peak - top_value) + jnp.exp(prior_lse - top_value)
    )
    loss = lse - all_target
    one_hot = (col_index[None, :] == column[:, None]).astype(jnp.float32)
    grad_logits = (jnp.exp(logits - lse[:, None]) - one_hot).astype(jnp.bfloat16)
    partial_value = jnp.dot(grad_logits, gathered, preferred_element_type=jnp.float32)
    hidden_grad = lax.psum_scatter(
        partial_value.astype(jnp.bfloat16), "tensor", scatter_dimension=1, tiled=True
    )
    return (loss, hidden_grad)


def solution(mesh):
    placed = (P("dp", "tensor"), P(("dp", "tensor"), None), P("dp"), P("dp"))
    return jax.shard_map(
        body, mesh=mesh, in_specs=placed, out_specs=(P("dp"), P("dp", "tensor")), check_vma=False
    )
```

profile of v0, /device:TPU:1, one launch (start us, length us, event | category | flops | bytes accessed | tf_op | source)
XLA Modules:
  0.0 371.6 jit_solution(15383345126242099963)
XLA Ops:
  7.2 0.0 copy-start
  7.2 0.0 all-gather.3.cloned.1.call-start
  7.2 0.7 all-gather.3.cloned.1.call-update
  7.9 0.0 all-gather.5.cloned.1.call-start
  8.0 0.7 all-gather.5.cloned.1.call-update
  8.7 0.0 reduce-scatter.2.cloned.1.call-start
  8.7 0.7 compare_select_fusion
  9.4 49.5 %all-gather.3.cloned.1.call-done = bf16[128,5376]{0,1:T(8,128)(2,1)} async-done(((bf16[128,1344]{0,1:T(8,128)(2,1)}), bf16[128,5376]{0,1:T(8,128)(2,1)}) %all-gather.3.cloned.1.call-update) | async-done | bytes 1376272 | tf_op jit(solution)/shard_map/all_gather | solution.py:8
  58.9 225.4 %all-gather.5.cloned.1.call-done = bf16[1024,5376]{1,0:T(8,128)(2,1)} async-done(((bf16[8,5376]{1,0:T(8,128)(2,1)}), bf16[1024,5376]{1,0:T(8,128)(2,1)}) %all-gather.5.cloned.1.call-update) | async-done | bytes 11010064 | tf_op jit(solution)/shard_map/all_gather | solution.py:16
  284.3 8.3 %fusion.6 = (f32[128]{0:T(128)S(1)}, f32[128,1024]{1,0:T(8,128)S(1)}) fusion(bf16[128,5376]{0,1:T(8,128)(2,1)} %all-gather.3.cloned.1.call-done, bf16[1024,5376]{1,0:T(8,128)(2,1)} %all-gather.5.cloned.1.call-done), kind=kOutput, calls=%fused_computation.25 | convolution fusion | flops 1409417088 | bytes 12911104 | tf_op jit(solution)/shard_map/td,vd->tv/dot_general | solution.py:17
  292.6 11.3 %pmax.7 = f32[128]{0:T(128)S(1)} all-reduce(f32[128]{0:T(128)S(1)} %get-tuple-element.8), channel_id=1, replica_groups=mesh['dp'=128,'tensor'=4] {'tensor'}, use_global_device_ids=true, to_apply=%region_1.2 | all-reduce | flops 128 | bytes 1024 | tf_op jit(solution)/shard_map/pmax | solution.py:22
  303.9 0.3 select_reduce_fusion
  304.2 7.3 %all-reduce = (f32[128]{0:T(128)S(1)}, f32[128]{0:T(128)S(1)}) all-reduce(f32[128]{0:T(128)S(1)} %exponential_multiply_fusion, f32[128]{0:T(128)S(1)} %get-tuple-element.2), channel_id=1, replica_groups=mesh['dp'=128,'tensor'=4] {'tensor'}, use_global_device_ids=true, to_apply=%region_3.4 | all-reduce | flops 256 | bytes 2048 | tf_op jit(solution)/shard_map/psum | solution.py:23
  311.5 0.0 copy-done
  311.5 0.5 fusion.5
  312.0 9.7 %convolution_convert_fusion = bf16[128,5376]{0,1:T(8,128)(2,1)} fusion(bf16[1024,5376]{1,0:T(8,128)(2,1)} %all-gather.5.cloned.1.call-done, f32[128,1024]{1,0:T(8,128)S(1)} %get-tuple-element.9, f32[128]{0:T(128)S(1)} %get-tuple-element.7, s32[128]{0:T(128)S(1)} %compare_select_fusion), kind=kOutput, calls=%fused_computation | convolution fusion | flops 1410629632 | bytes 12911616 | tf_op jit(solution)/shard_map/dot_general | solution.py:33
  321.7 0.0 reduce-scatter.2.cloned.1.call-update
  321.7 43.3 %reduce-scatter.2.cloned.1.call-done = bf16[128,1344]{0,1:T(8,128)(2,1)} async-done(((bf16[128,5376]{0,1:T(8,128)(2,1)}), bf16[128,1344]{0,1:T(8,128)(2,1)}) %reduce-scatter.2.cloned.1.call-update) | async-done | bytes 344080 | tf_op jit(solution)/shard_map/reduce_scatter | solution.py:34
  (1 shorter events, 0.0 us)
Async XLA Ops:
  7.2 304.4 %copy-start = (f32[128]{0:T(128)S(1)}, f32[128]{0:T(128)}, u32[]{:S(2)}) copy-start(f32[128]{0:T(128)} %param.7) | copy-start | bytes 1540
  7.2 51.7 %all-gather.3.cloned.1.call-start = ((), (), s32[]{:S(2)}) async-start(), calls=%async_computation.1 | async-start | bytes 1720320 | tf_op jit(solution)/shard_map/all_gather | solution.py:8
  7.9 276.4 %all-gather.5.cloned.1.call-start = ((), (), s32[]{:S(2)}) async-start(), calls=%async_computation.2 | async-start | bytes 11096064 | tf_op jit(solution)/shard_map/all_gather | solution.py:16
  8.7 356.4 %reduce-scatter.2.cloned.1.call-start = ((), (), s32[]{:S(2)}) async-start(), calls=%async_computation.3 | async-start | bytes 1720320 | tf_op jit(solution)/shard_map/reduce_scatter | solution.py:34
Sparse Core Ops, SparseCore 0:
  10.1 48.7 all-gather.2
  61.1 223.2 all-gather.4
  321.8 43.1 reduce-scatter.1
where the time goes:
time: 372 us
  waiting for transfers between devices  320 us (86%)
  blocking collectives  18.6 us (5%)
  matrix products  17.9 us (5%)
  between operations  13.8 us (4%)
    all_gather x1, waiting for transfers between devices, body(): gathered = lax.all_gather(embedding, 'dp', axis=0, tiled=True)  225 us
    all_gather x1, waiting for transfers between devices, body(): hidden = lax.all_gather(hidden_states, 'tensor', axis=1, tiled=True)  49.5 us
    reduce_scatter x1, waiting for transfers between devices, body(): lax.psum_scatter(partial_value.astype(jnp.bfloat16), 'tensor', scatter_di...  43.3 us
    pmax x1, blocking collectives, body(): all_peak = lax.pmax(row_peak, 'tensor')  11.3 us
    dot_general x1, matrix products, body(): jnp.dot(grad_logits, gathered, preferred_element_type=jnp.float32)  9.65 us
    dot_general x1, matrix products, body(): jnp.einsum('td,vd->tv', hidden, gathered, preferred_element_type=jnp.floa...  8.29 us
  transfers between devices with their start and end apart: 3, of which 3 were waited for; matrix products, arithmetic and copies ran while one was open for 0% of the time, Pallas kernels for 0%

commit v1 on v0

v1 whole, which is shorter than its diff:
```python
import jax
import jax.numpy as jnp
from jax import lax
from jax.experimental import pallas as pl
from jax.experimental.pallas import tpu as pltpu
from jax.sharding import PartitionSpec as P

MESH = pl.DeviceIdType.MESH
BF16 = jnp.bfloat16
F32 = jnp.float32
NX, NY, NZ, NK = 4, 8, 8, 4
D = 5376
QUARTER = D // NK
HALF = D // 2
TOK = 128
SET = TOK // NK
PIECE = 16
BLOCK = 8 * PIECE
ROWS = NY * NZ * PIECE


def device(x, y, z, c):
    return (((z % 2) * NX + x) * NY + y) * 2 + c, z // 2


def at_row(row):
    return pl.ds(pl.multiple_of(row * PIECE, PIECE), PIECE)


def ring_offset(m):
    return ((m + 1) // 2) * (1 - 2 * (m % 2))


def kernel(
    hid, emb, tgt, pri, loss, out,
    g, ebuf, hb, ht, lt, gl, meta, stat, lbuf, part, r1, s2, r2, zs, zr,
    e_s, g_r, s_r, p1_s, p2_s, s_s, ha_s, ha_r, hx_s, hx_r, hr_s, hr_r,
    m_s, m_r, t_s, t_r, l_s, l_r, o_s, o_r, d_s, d_r, q_s, q_r, z_s, z_r,
):
    dp = lax.axis_index("dp")
    k = lax.axis_index("tensor")
    c = dp % 2
    y = dp // 2 % NY
    x = dp // (2 * NY) % NX
    zl = dp // (2 * NY * NX)
    z = 2 * k + zl
    first = c == 0

    def x_dev(d):
        return device((x + d) % NX, y, z, c)

    def k_dev(kk):
        return device(x, y, 2 * kk + zl, c)

    sibling = device(x, y, z, 1 - c)

    outer, inner = jnp.where(first, z, y), jnp.where(first, y, z)

    def ring_dev(o, i):
        return device(x, jnp.where(first, i, o), jnp.where(first, o, i), c)

    inner_next = ring_dev(outer, (inner + 1) % 8)
    inner_last = ring_dev(outer, (inner + 7) % 8)
    outer_next = ring_dev((outer + 1) % 8, inner)
    outer_last = ring_dev((outer + 7) % 8, inner)

    partners = [sibling, inner_next, inner_last, outer_next, outer_last]
    partners += [x_dev(d) for d in (1, 2, 3)] + [k_dev((k + d) % NK) for d in (1, 2, 3)]
    barrier = pltpu.get_barrier_semaphore()
    for partner in partners:
        pl.semaphore_signal(barrier, inc=1, device_id=partner, device_id_type=MESH)
    pl.semaphore_wait(barrier, len(partners))

    def copy(src, dst, send, recv, where):
        return pltpu.make_async_remote_copy(
            src_ref=src, dst_ref=dst, send_sem=send, recv_sem=recv,
            device_id=where, device_id_type=MESH,
        )

    e_copy = copy(emb, ebuf, e_s.at[0], e_s.at[1], sibling)
    e_copy.start()

    def set_rows(kk):
        return pl.ds(pl.multiple_of(kk * SET, SET), SET)

    def hidden_set(d):
        kk = (k + d) % NK
        return copy(hid.at[set_rows(kk)], hb.at[x, k], ha_s.at[d - 1], ha_r.at[d - 1], k_dev(kk))

    for d in (2, 1, 3):
        hidden_set(d).start()
    hb[x, k] = hid[set_rows(k), :]

    def hidden_x(j, way):
        ref = hb.at[x, j]
        return copy(ref, ref, hx_s.at[way, j], hx_r.at[way, j], x_dev(1 - 2 * way + NX))

    for way in (0, 1):
        hidden_x(k, way).start()

    t = tgt[...]
    b = t // 8
    t_dp, t_k = b // 4, b % 4
    t_z = 2 * t_k + t_dp // (2 * NY * NX)
    place = (t_dp // (2 * NY) % NX) * ROWS + (t_z * NY + t_dp // 2 % NY) * PIECE + t_dp % 2 * 8 + t % 8
    meta[x] = jnp.concatenate([place.astype(F32), pri[...], jnp.zeros((6, TOK), F32)], axis=0)

    def to_x(buf, send, recv, d):
        return copy(buf.at[x], buf.at[x], send.at[d - 1], recv.at[d - 1], x_dev(d))

    for d in (1, 2, 3):
        to_x(meta, m_s, m_r, d).start()

    e_copy.wait()
    mine, other = emb[...], ebuf[...]
    rows = jnp.concatenate(
        [jnp.where(first, mine, other), jnp.where(first, other, mine)], axis=0
    )
    g[0, at_row(z * NY + y), :] = rows[:, :HALF]
    g[1, at_row(y * NZ + z), :] = rows[:, HALF:]

    def piece(o, i):
        return g.at[c, at_row(o * 8 + i)]

    def from_ring(o, i):
        ref = piece(o, i)
        copy(ref, ref, e_s.at[0], g_r.at[o * 8 + i], outer_next).wait_recv()

    def to_ring(o, i, send, where):
        ref = piece(o, i)
        return copy(ref, ref, send, g_r.at[o * 8 + i], where)

    def to_sibling(o, i):
        ref = piece(o, i)
        return copy(ref, ref, s_s.at[o * 8 + i], s_r.at[o * 8 + i], sibling)

    def from_sibling(o, i):
        ref = g.at[1 - c, at_row(o * 8 + i)]
        copy(ref, ref, s_s.at[0], s_r.at[o * 8 + i], sibling).wait_recv()

    def to_outer(m):
        i = (inner + ring_offset(m) + 8) % 8
        to_ring(outer, i, p2_s.at[0, m], outer_next).start()
        to_ring(outer, i, p2_s.at[1, m], outer_last).start()

    to_ring(outer, inner, p1_s.at[0, 0], inner_next).start()
    to_ring(outer, inner, p1_s.at[1, 0], inner_last).start()
    to_outer(0)
    for s in range(1, 5):
        i = (inner + 8 - s) % 8
        from_ring(outer, i)
        if s < 4:
            to_ring(outer, i, p1_s.at[0, s], inner_next).start()
        to_outer(2 * s - 1)
        to_sibling(outer, i).start()
        if s < 4:
            i = (inner + s) % 8
            from_ring(outer, i)
            if s < 3:
                to_ring(outer, i, p1_s.at[1, s], inner_last).start()
            to_outer(2 * s)
            to_sibling(outer, i).start()

    def second(ring, last):
        up, down = (outer + 8 - ring) % 8, (outer + ring) % 8

        def step(m, carry):
            i = (inner + ring_offset(m) + 8) % 8

            def pass_on(o, way, where):
                to_ring(o, i, p2_s.at[way, ring * 8 + m], where).start()

            from_ring(up, i)
            if last:
                pl.when(m < 4)(lambda: pass_on(up, 0, outer_next))
            else:
                pass_on(up, 0, outer_next)
            to_sibling(up, i).start()
            from_ring(down, i)
            if last:
                pl.when(m >= 4)(lambda: pass_on(down, 1, outer_last))
            else:
                pass_on(down, 1, outer_last)
            to_sibling(down, i).start()
            return carry

        lax.fori_loop(0, 8, step, 0)

    for d in (2, 1, 3):
        hidden_set(d).wait()
        for way in (0, 1):
            hidden_x((k + NK - d) % NK, way).start()

    second(1, False)

    def hidden_pass(j):
        way = j // 2
        ref = hb.at[(x + NX - 1 + 2 * way) % NX, j]
        return copy(ref, ref, hr_s.at[j], hr_r.at[j], x_dev(1 - 2 * way + NX))

    for j in range(NK):
        for way in (0, 1):
            hidden_x(j, way).wait()
        hidden_pass(j).start()

    second(2, False)

    for j in range(NK):
        hidden_pass(j).wait()
    for xx in range(NX):
        for h in (0, 1):
            ht[h, xx * SET:(xx + 1) * SET, :] = jnp.concatenate(
                [hb[xx, 2 * h], hb[xx, 2 * h + 1]], axis=1
            )

    def logits(h, o):
        where = pl.ds(pl.multiple_of(o * BLOCK, BLOCK), BLOCK)
        lt[h, where, :] = lax.dot_general(
            g[h, where, :], ht[h], (((1,), (1,)), ((), ())), preferred_element_type=F32
        )

    def sibling_block(r):
        o = (inner + r) % 8

        def wait(m, carry):
            i = (outer + m) % 8
            pl.when((r != 0) | (m != 0))(lambda: from_sibling(o, i))
            return carry

        lax.fori_loop(0, 8, wait, 0)
        logits(1 - c, o)

    def early(n, carry):
        r = (n + 6) % 8
        logits(c, (outer + r) % 8)
        sibling_block(r)
        return carry

    lax.fori_loop(0, 5, early, 0)

    second(3, True)

    across = (outer + 4) % 8

    def final(m, carry):
        i = (inner + ring_offset(m) + 8) % 8
        from_ring(across, i)
        to_sibling(across, i).start()
        return carry

    for m in (0, 4, 1, 5, 2, 6, 3, 7):
        final(m, 0)

    def late(n, carry):
        r = n + 3
        logits(c, (outer + r) % 8)
        sibling_block(r)
        return carry

    lax.fori_loop(0, 3, late, 0)

    lane_set = lax.broadcasted_iota(jnp.int32, (8, TOK), 1) // SET
    for d in (1, 2, 3):
        to_x(meta, m_s, m_r, d).wait()
    info = jnp.zeros((8, TOK), F32)
    for xx in range(NX):
        turned = pltpu.roll(meta[xx], (xx + NX - k) % NX * SET, axis=1)
        info = jnp.where(lane_set == xx, turned, info)
    column = info[0:1] - (x * ROWS).astype(F32)
    prior = info[1:2]

    peak = jnp.full((1, TOK), -jnp.inf, F32)
    for zz in range(NZ):
        for yy in range(NY):
            r0, r1_ = (zz * NY + yy) * PIECE, (yy * NZ + zz) * PIECE
            value = lt[0, r0:r0 + PIECE, :] + lt[1, r1_:r1_ + PIECE, :]
            lt[0, r0:r0 + PIECE, :] = value
            peak = jnp.maximum(peak, jnp.max(value, axis=0, keepdims=True))
    total = jnp.zeros((8, TOK), F32)
    target = jnp.zeros((8, TOK), F32)
    row_id = lax.broadcasted_iota(jnp.int32, (BLOCK, TOK), 0).astype(F32)
    for n in range(8):
        value = lt[0, n * BLOCK:(n + 1) * BLOCK, :]
        hit = row_id == column - float(n * BLOCK)
        power = jnp.exp(value - peak)
        lt[0, n * BLOCK:(n + 1) * BLOCK, :] = power
        total += jnp.sum(power.reshape(BLOCK // 8, 8, TOK), axis=0)
        target += jnp.sum(jnp.where(hit, value, 0.0).reshape(BLOCK // 8, 8, TOK), axis=0)
    stat[x] = jnp.concatenate(
        [peak, jnp.sum(total, axis=0, keepdims=True), jnp.sum(target, axis=0, keepdims=True),
         jnp.zeros((5, TOK), F32)], axis=0,
    )
    for d in (1, 2, 3):
        to_x(stat, t_s, t_r, d).start()
    for d in (1, 2, 3):
        to_x(stat, t_s, t_r, d).wait()
    top = prior
    for xx in range(NX):
        top = jnp.maximum(top, stat[xx, 0:1, :])
    whole = jnp.exp(prior - top)
    logit = jnp.zeros((1, TOK), F32)
    for xx in range(NX):
        whole += stat[xx, 1:2, :] * jnp.exp(stat[xx, 0:1, :] - top)
        logit += stat[xx, 2:3, :]
    lse = top + jnp.log(whole)
    lbuf[k] = jnp.broadcast_to(lse - logit, (8, TOK))

    def loss_to(d):
        return copy(lbuf.at[k], lbuf.at[k], l_s.at[d - 1], l_r.at[d - 1], k_dev((k + d) % NK))

    for d in (1, 2, 3):
        loss_to(d).start()

    scale = jnp.exp(peak - lse)
    for n in range(8):
        hit = row_id == column - float(n * BLOCK)
        value = lt[0, n * BLOCK:(n + 1) * BLOCK, :] * scale - jnp.where(hit, 1.0, 0.0)
        gl[0, :, n * BLOCK:(n + 1) * BLOCK] = value.T.astype(BF16)
        for yy in range(NY):
            r = (yy * NZ + n) * PIECE
            lt[1, r:r + PIECE, :] = value[yy * PIECE:(yy + 1) * PIECE]
    for n in range(8):
        gl[1, :, n * BLOCK:(n + 1) * BLOCK] = lt[1, n * BLOCK:(n + 1) * BLOCK, :].T.astype(BF16)

    def x_rows(d):
        return pl.ds(pl.multiple_of((x + d) % NX * SET, SET), SET)

    half_order = [1 - k // 2, k // 2]

    def quarter(n):
        return 2 * half_order[n // 2] + n % 2

    def ahead(n):
        return 1 if n % 2 == 0 else 3

    def opposite_copy(n):
        j = quarter(n)
        return copy(part.at[j, x_rows(2)], r1.at[j], o_s.at[n], o_r.at[n], x_dev(ahead(n)))

    def direct_copy(n):
        j, d = quarter(n), 4 - ahead(n)
        return copy(part.at[j, x_rows(d)], r2.at[0, j], d_s.at[n], d_r.at[n], x_dev(d))

    def sum_copy(n):
        j = quarter(n)
        return copy(s2.at[j], r2.at[1, j], q_s.at[n], q_r.at[n], x_dev(ahead(n)))

    def z_copy(n):
        j = quarter(n)
        return copy(zs.at[j], zr.at[k], z_s.at[n], z_r.at[k], k_dev(j))

    def multiply(n):
        h, j = half_order[n // 2], quarter(n)
        lo = 0 if n % 2 == 0 else HALF - 1408
        value = jnp.dot(gl[h], g[h, :, lo:lo + 1408], preferred_element_type=F32).astype(BF16)
        part[j] = value[:, :QUARTER] if n % 2 == 0 else value[:, 1408 - QUARTER:]
        opposite_copy(n).start()
        direct_copy(n).start()

    def add_first(n):
        j = quarter(n)
        opposite_copy(n).wait()
        s2[j] = (part[j, x_rows(ahead(n)), :].astype(F32) + r1[j].astype(F32)).astype(BF16)
        sum_copy(n).start()

    def add_last(n):
        j = quarter(n)
        direct_copy(n).wait()
        sum_copy(n).wait()
        value = part[j, x_rows(0), :].astype(F32) + r2[0, j].astype(F32) + r2[1, j].astype(F32)
        zs[j] = value.astype(BF16)

        @pl.when(j == k)
        def _():
            zr[k] = value.astype(BF16)

        @pl.when(j != k)
        def _():
            z_copy(n).start()

    multiply(0)
    multiply(1)
    add_first(0)
    multiply(2)
    add_first(1)
    multiply(3)
    add_first(2)
    add_last(0)
    add_first(3)
    add_last(1)
    add_last(2)
    add_last(3)

    for d in (1, 2, 3):
        loss_to(d).wait()
    result = jnp.zeros((8, TOK), F32)
    for kk in range(NK):
        turned = pltpu.roll(lbuf[kk], (kk + NX - x) % NX * SET, axis=1)
        result = jnp.where(lane_set == kk, turned, result)
    loss[...] = result[0:1]

    for n in range(NK):
        @pl.when(quarter(n) != k)
        def _():
            z_copy(n).wait_send()
    for d in (1, 2, 3):
        kk = (k + d) % NK
        copy(zr.at[kk], zr.at[kk], z_s.at[0], z_r.at[kk], k_dev(kk)).wait_recv()
    for kk in range(NK):
        out[kk * SET:(kk + 1) * SET, :] = zr[kk]

    def sent(send):
        ref = piece(outer, inner)
        copy(ref, ref, send, g_r.at[0], outer_next).wait_send()

    for s in range(4):
        sent(p1_s.at[0, s])
        if s < 3:
            sent(p1_s.at[1, s])

    def sent_second(n, carry):
        sent(p2_s.at[0, n])
        sent(p2_s.at[1, n])
        return carry

    lax.fori_loop(0, 24, sent_second, 0)
    for m in range(4):
        sent(p2_s.at[0, 24 + m])
        sent(p2_s.at[1, 28 + m])

    def sent_sibling(n, carry):
        pl.when(n != outer * 8 + inner)(lambda: sent(s_s.at[n]))
        return carry

    lax.fori_loop(0, 64, sent_sibling, 0)


def body(hidden_states, embedding, targets, prior_lse):
    dma = pltpu.SemaphoreType.DMA
    vmem = pl.BlockSpec(memory_space=pltpu.VMEM)
    loss, grad = pl.pallas_call(
        kernel,
        out_shape=(
            jax.ShapeDtypeStruct((1, TOK), F32),
            jax.ShapeDtypeStruct((TOK, QUARTER), BF16),
        ),
        in_specs=[vmem] * 4,
        out_specs=(vmem, vmem),
        scratch_shapes=[
            pltpu.VMEM((2, ROWS, HALF), BF16),
            pltpu.VMEM((8, D), BF16),
            pltpu.VMEM((NX, NK, SET, QUARTER), BF16),
            pltpu.VMEM((2, TOK, HALF), BF16),
            pltpu.VMEM((2, ROWS, TOK), F32),
            pltpu.VMEM((2, TOK, ROWS), BF16),
            pltpu.VMEM((NX, 8, TOK), F32),
            pltpu.VMEM((NX, 8, TOK), F32),
            pltpu.VMEM((NK, 8, TOK), F32),
            pltpu.VMEM((NK, TOK, QUARTER), BF16),
            pltpu.VMEM((NK, SET, QUARTER), BF16),
            pltpu.VMEM((NK, SET, QUARTER), BF16),
            pltpu.VMEM((2, NK, SET, QUARTER), BF16),
            pltpu.VMEM((NK, SET, QUARTER), BF16),
            pltpu.VMEM((NK, SET, QUARTER), BF16),
            dma((2,)), dma((64,)), dma((64,)), dma((2, 4)), dma((2, 32)), dma((64,)),
            dma((3,)), dma((3,)), dma((2, 4)), dma((2, 4)), dma((4,)), dma((4,)),
            dma((3,)), dma((3,)), dma((3,)), dma((3,)), dma((3,)), dma((3,)),
            dma((4,)), dma((4,)), dma((4,)), dma((4,)), dma((4,)), dma((4,)), dma((4,)), dma((4,)),
        ],
        compiler_params=pltpu.CompilerParams(
            collective_id=0, has_side_effects=True, vmem_limit_bytes=48 << 20
        ),
        cost_estimate=pl.CostEstimate(
            flops=4 * TOK * ROWS * D, bytes_accessed=4 * TOK * D, transcendentals=TOK * ROWS
        ),
    )(hidden_states, embedding, targets.reshape(1, TOK), prior_lse.reshape(1, TOK))
    return loss.reshape(TOK), grad


def solution(mesh):
    placed = (P("dp", "tensor"), P(("dp", "tensor"), None), P("dp"), P("dp"))
    return jax.shard_map(
        body, mesh=mesh, in_specs=placed, out_specs=(P("dp"), P("dp", "tensor")), check_vma=False
    )
```

time: 372 us -> 94.1 us (0.25)
  the two profiles are of different devices: /device:TPU:1 before, /device:TPU:17 now
where the time goes in v1:
time: 94.1 us; the launch traced here: 94 us
  Pallas kernels  90.6 us (96%)
  local copies, waits for them, and re-layouts  2.65 us (3%)
    pallas_call x1, Pallas kernels, body(): pl.pallas_call(kernel, out_shape=(jax.ShapeDtypeStruct((1, TOK), F32), ja...  90.6 us
    unnamed x9, local copies, waits for them, and re-layouts  2.65 us

profile of v1, /device:TPU:17, one launch (start us, length us, event | category | flops | bytes accessed | tf_op | source)
XLA Modules:
  0.0 94.0 jit_solution(12787370406991695532)
XLA Ops:
  0.6 0.0 copy-start
  0.6 0.0 copy-start.1
  0.7 0.0 copy-start.2
  0.7 1.2 %copy.6.hid = bf16[128,1344]{1,0:T(8,128)(2,1)S(1)} copy(bf16[128,1344]{0,1:T(8,128)(2,1)} %param.4) | data formatting | bytes 688128 | tf_op args[0]
  1.9 0.0 copy-done
  1.9 0.0 copy-done.1
  1.9 0.0 copy-done.2
  1.9 90.6 %shard_map.59 = (f32[1,128]{1,0:T(1,128)S(1)}, bf16[128,1344]{1,0:T(8,128)(2,1)S(1)}) custom-call(bf16[128,1344]{1,0:T(8,128)(2,1)S(1)} %copy.6.hid, bf16[8,5376]{1,0:T(8,128)(2,1)S(1)} %copy-done, s32[1,128]{1,0:T(1,128)S(1)} %bitcast.3, f32[1,128]{1,0:T(1,128)S(1)} %bitcast.4), custom_call_target="tpu_custom_call" | custom-call | flops 2818572288 | bytes 2752512 | tf_op jit(solution)/shard_map/pallas_call | solution.py:441
  92.6 0.9 copy.7
  93.5 0.5 copy.9
Async XLA Ops:
  0.6 1.3 %copy-start = (bf16[8,5376]{1,0:T(8,128)(2,1)S(1)}, bf16[8,5376]{1,0:T(8,128)(2,1)}, u32[]{:S(2)}) copy-start(bf16[8,5376]{1,0:T(8,128)(2,1)} %emb.1) | copy-start | bytes 258052
  0.6 1.3 %copy-start.1 = (s32[128]{0:T(128)S(1)}, s32[128]{0:T(128)}, u32[]{:S(2)}) copy-start(s32[128]{0:T(128)} %param.6) | copy-start | bytes 1540
  0.7 1.3 %copy-start.2 = (f32[128]{0:T(128)S(1)}, f32[128]{0:T(128)}, u32[]{:S(2)}) copy-start(f32[128]{0:T(128)} %param.7) | copy-start | bytes 1540

commit v2 on v0

v2 whole, which is shorter than its diff:
```python
import functools

import jax
import jax.numpy as jnp
from jax import lax
from jax.experimental import pallas as pl
from jax.experimental.pallas import tpu as pltpu
from jax.sharding import PartitionSpec as P

MESH = pl.DeviceIdType.MESH
BF16 = jnp.bfloat16
F32 = jnp.float32
NX, NY, NZ, NK = 4, 8, 8, 4
D = 5376
QUARTER = D // NK
MAIN = QUARTER // 128 * 128
REST = QUARTER - MAIN
SPLIT = 19 * 128
TOK = 128
SET = TOK // NK
SUB = SET // 2
PIECE = 16
BLOCK = 8 * PIECE
ROWS = NY * NZ * PIECE


def device(x, y, z, c):
    return (((z % 2) * NX + x) * NY + y) * 2 + c, z // 2


def at_row(row):
    return pl.ds(pl.multiple_of(row * PIECE, PIECE), PIECE)


def ring_offset(m):
    return ((m + 1) // 2) * (1 - 2 * (m % 2))


def rearranged(quarters):
    return jnp.concatenate(
        [q[:, :MAIN] for q in quarters] + [q[:, MAIN:] for q in quarters], axis=1
    )


def kernel(
    hid, emb, tgt, pri, loss, out,
    g, ebuf, hidn, hb, ht, lt, gl, raw, coef, meta, stat, lbuf, part, r1, s2, rd, rs, r3, zs, zr,
    e_s, g_r, s_r, g_s, s_s, ha_s, ha_r, hx_s, hx_r,
    m_s, m_r, t_s, t_r, l_s, l_r, o_s, o_r, d_s, d_r, q_s, q_r, w_s, w_r, z_s, z_r,
):
    dp = lax.axis_index("dp")
    k = lax.axis_index("tensor")
    c = dp % 2
    y = dp // 2 % NY
    x = dp // (2 * NY) % NX
    zl = dp // (2 * NY * NX)
    z = 2 * k + zl

    def x_dev(d):
        return device((x + d) % NX, y, z, c)

    def k_dev(kk):
        return device(x, y, 2 * kk + zl, c)

    sibling = device(x, y, z, 1 - c)

    partners = [sibling]
    partners += [device(x, (y + d) % NY, z, c) for d in (1, 7)]
    partners += [device(x, y, (z + d) % NZ, c) for d in (1, 7)]
    partners += [x_dev(d) for d in (1, 2, 3)] + [k_dev((k + d) % NK) for d in (1, 2, 3)]
    barrier = pltpu.get_barrier_semaphore()
    for partner in partners:
        pl.semaphore_signal(barrier, inc=1, device_id=partner, device_id_type=MESH)

    for lo in range(0, QUARTER, 128):
        hi = min(lo + 128, QUARTER)
        hidn[:, lo:hi] = hid[lo:hi, :].astype(F32).T.astype(BF16)
    t = tgt[...]
    b = t // 8
    t_dp, t_k = b // 4, b % 4
    t_z = 2 * t_k + t_dp // (2 * NY * NX)
    place = (t_dp // (2 * NY) % NX) * ROWS + (t_z * NY + t_dp // 2 % NY) * PIECE + t_dp % 2 * 8 + t % 8
    meta[x] = jnp.concatenate([place.astype(F32), pri[...], jnp.zeros((6, TOK), F32)], axis=0)
    pl.semaphore_wait(barrier, len(partners))

    def copy(src, dst, send, recv, where):
        return pltpu.make_async_remote_copy(
            src_ref=src, dst_ref=dst, send_sem=send, recv_sem=recv,
            device_id=where, device_id_type=MESH,
        )

    e_copy = copy(emb, ebuf, e_s.at[0], e_s.at[1], sibling)
    e_copy.start()

    def set_rows(kk):
        return pl.ds(pl.multiple_of(kk * SET, SET), SET)

    def hidden_set(d):
        kk = (k + d) % NK
        return copy(hidn.at[set_rows(kk)], hb.at[x, k], ha_s.at[d - 1], ha_r.at[d - 1], k_dev(kk))

    def hidden_x(j, d):
        ref = hb.at[x, j]
        return copy(ref, ref, hx_s.at[d - 1, j], hx_r.at[d - 1, j], x_dev(d))

    def hidden_on(d):
        hidden_set(d).wait()
        for e in (1, 3, 2):
            hidden_x((k + NK - d) % NK, e).start()

    def to_x(buf, send, recv, d):
        return copy(buf.at[x], buf.at[x], send.at[d - 1], recv.at[d - 1], x_dev(d))

    hb[x, k] = hidn[set_rows(k), :]
    e_copy.wait()
    mine, other = emb[...], ebuf[...]
    rows = jnp.concatenate(
        [jnp.where(c == 0, mine, other), jnp.where(c == 0, other, mine)], axis=0
    )
    g[at_row(z * NY + y), :] = rearranged(
        [rows[:, j * QUARTER:(j + 1) * QUARTER] for j in range(NK)]
    )

    def bring_in(h):
        outer, inner = (z, y) if h == 0 else (y, z)
        spans = (slice(0, SPLIT), slice(SPLIT, D))

        def number(o, i):
            return o * 8 + i if h == 0 else i * 8 + o

        def ring_dev(o, i):
            return device(x, i, o, c) if h == 0 else device(x, o, i, c)

        inner_next = ring_dev(outer, (inner + 1) % 8)
        inner_last = ring_dev(outer, (inner + 7) % 8)
        outer_next = ring_dev((outer + 1) % 8, inner)
        outer_last = ring_dev((outer + 7) % 8, inner)

        def piece(n, share):
            return g.at[at_row(n), spans[share]]

        def from_ring(o, i):
            ref = piece(number(o, i), h)
            copy(ref, ref, g_s.at[0], g_r.at[number(o, i)], outer_next).wait_recv()

        def to_ring(o, i, where):
            ref = piece(number(o, i), h)
            copy(ref, ref, g_s.at[0], g_r.at[number(o, i)], where).start()

        def to_sibling(o, i):
            ref = piece(number(o, i), h)
            copy(ref, ref, s_s.at[0], s_r.at[number(o, i)], sibling).start()

        def to_outer(m):
            i = (inner + ring_offset(m) + 8) % 8
            to_ring(outer, i, outer_next)
            to_ring(outer, i, outer_last)

        to_ring(outer, inner, inner_next)
        to_ring(outer, inner, inner_last)
        to_outer(0)
        for e in (1, 3, 2):
            hidden_x(k, e).start()
        for d in (1, 3, 2):
            hidden_set(d).start()
        for d in (1, 2, 3):
            to_x(meta, m_s, m_r, d).start()
        for s in range(1, 5):
            i = (inner + 8 - s) % 8
            from_ring(outer, i)
            if s < 4:
                to_ring(outer, i, inner_next)
            to_outer(2 * s - 1)
            to_sibling(outer, i)
            if s < 4:
                i = (inner + s) % 8
                from_ring(outer, i)
                if s < 3:
                    to_ring(outer, i, inner_last)
                to_outer(2 * s)
                to_sibling(outer, i)
            if s == 2:
                hidden_on(1)
                hidden_on(3)
            if s == 3:
                hidden_on(2)

        def second(ring, first, end):
            up, down = (outer + 8 - ring) % 8, (outer + ring) % 8

            def step(m, carry):
                i = (inner + ring_offset(m) + 8) % 8
                from_ring(up, i)
                if ring == 3:
                    pl.when(m < 4)(lambda: to_ring(up, i, outer_next))
                else:
                    to_ring(up, i, outer_next)
                to_sibling(up, i)
                from_ring(down, i)
                if ring == 3:
                    pl.when(m >= 4)(lambda: to_ring(down, i, outer_last))
                else:
                    to_ring(down, i, outer_last)
                to_sibling(down, i)
                return carry

            lax.fori_loop(first, end, step, 0)

        def logits(share, offsets):
            o0 = outer if share == h else inner
            by_z = share == 0
            starts = []
            for r in offsets:
                o = (o0 + r) % 8
                if by_z:
                    starts.append((pl.multiple_of(o * BLOCK, BLOCK), BLOCK))
                else:
                    starts += [(pl.multiple_of((i * 8 + o) * PIECE, PIECE), PIECE) for i in range(8)]
            left = jnp.concatenate([g[pl.ds(a, n), spans[share]] for a, n in starts], axis=0)
            value = lax.dot_general(
                left, ht[:, spans[share]], (((1,), (1,)), ((), ())), preferred_element_type=F32
            )
            at = 0
            for a, n in starts:
                lt[share, pl.ds(a, n), :] = value[at:at + n]
                at += n

        def await_sibling(r, skip):
            o = (inner + r) % 8

            def wait(m, carry):
                n = number((outer + m) % 8, o)
                ref = piece(n, 1 - h)
                copy(ref, ref, s_s.at[0], s_r.at[n], sibling).wait_recv()
                return carry

            lax.fori_loop(skip, 8, wait, 0)

        second(1, 0, 8)
        second(2, 0, 8)
        for j in range(NK):
            for d in (1, 2, 3):
                hidden_x(j, d).wait()
        for xx in range(NX):
            ht[xx * SET:(xx + 1) * SET, :] = rearranged([hb[xx, j] for j in range(NK)])

        def early(r, carry):
            second(3, 4 * (r - 1), 4 * r)
            logits(h, (r, 8 - r))
            await_sibling(r, 0)
            await_sibling(8 - r, 0)
            logits(1 - h, (r, 8 - r))
            return carry

        lax.fori_loop(1, 3, early, 0)
        logits(h, (3, 5))
        logits(h, (0,))
        await_sibling(0, 1)
        logits(1 - h, (0,))
        await_sibling(3, 0)
        await_sibling(5, 0)
        logits(1 - h, (3, 5))
        across = (outer + 4) % 8
        for m in (0, 4, 1, 5, 2, 6, 3, 7):
            i = (inner + ring_offset(m) + 8) % 8
            from_ring(across, i)
            to_sibling(across, i)
        logits(h, (4,))
        await_sibling(4, 0)
        logits(1 - h, (4,))

        ref = g.at[0:ROWS - PIECE, spans[h]]
        copy(ref, ref, g_s.at[0], g_r.at[0], outer_next).wait_send()
        copy(ref, ref, s_s.at[0], s_r.at[0], sibling).wait_send()

    for core in (0, 1):
        pl.when(c == core)(functools.partial(bring_in, core))

    lane_set = lax.broadcasted_iota(jnp.int32, (8, TOK), 1) // SET
    for d in (1, 2, 3):
        to_x(meta, m_s, m_r, d).wait()
    info = jnp.zeros((8, TOK), F32)
    for xx in range(NX):
        turned = pltpu.roll(meta[xx], (xx + NX - k) % NX * SET, axis=1)
        info = jnp.where(lane_set == xx, turned, info)
    column = info[0:1] - (x * ROWS).astype(F32)
    owned = (column >= 0.0) & (column < float(ROWS))
    prior = info[1:2]

    peaks = jnp.full((8, TOK), -jnp.inf, F32)
    for n in range(8):
        span = slice(n * BLOCK, (n + 1) * BLOCK)
        value = lt[0, span, :] + lt[1, span, :]
        lt[0, span, :] = value
        peaks = jnp.maximum(peaks, jnp.max(value.reshape(BLOCK // 8, 8, TOK), axis=0))
    peak = jnp.max(peaks, axis=0, keepdims=True)
    total = jnp.zeros((8, TOK), F32)
    target = jnp.zeros((8, TOK), F32)
    row_id = lax.broadcasted_iota(jnp.int32, (BLOCK, TOK), 0).astype(F32)
    for n in range(8):
        span = slice(n * BLOCK, (n + 1) * BLOCK)
        value = lt[0, span, :]
        hit = row_id == column - float(n * BLOCK)
        power = jnp.exp(value - peak)
        lt[1, span, :] = jnp.where(hit, 0.0, power)
        total += jnp.sum(power.reshape(BLOCK // 8, 8, TOK), axis=0)
        target += jnp.sum(jnp.where(hit, value, 0.0).reshape(BLOCK // 8, 8, TOK), axis=0)
    my_target = jnp.sum(target, axis=0, keepdims=True)
    stat[x] = jnp.concatenate(
        [peak, jnp.sum(total, axis=0, keepdims=True), my_target, jnp.zeros((5, TOK), F32)], axis=0
    )
    for d in (1, 2, 3):
        to_x(stat, t_s, t_r, d).start()

    column_t = jnp.broadcast_to(column, (8, TOK)).T[:, 0:1]
    lane_id = lax.broadcasted_iota(jnp.int32, (TOK, BLOCK), 1).astype(F32)
    for n in range(8):
        span = slice(n * BLOCK, (n + 1) * BLOCK)
        gl[0:TOK, span] = lt[1, span, :].T.astype(BF16)
        gl[TOK:, span] = jnp.where(lane_id == column_t - float(n * BLOCK), 1.0, 0.0).astype(BF16)

    quarters = [(k + 2) % NK, (k + 1) % NK, (k + 3) % NK, k]

    def products(n, use):
        j = quarters[n]
        for lo in range(0, MAIN, 256):
            at = pl.ds(pl.multiple_of(j * MAIN + lo, 128), 256)
            use(lo, jnp.dot(gl[...], g[:, at], preferred_element_type=F32))
        at = pl.ds(pl.multiple_of(NK * MAIN + j // 2 * 128, 128), 128)
        value = jnp.dot(gl[...], g[:, at], preferred_element_type=F32)
        use(MAIN, pltpu.roll(value, j % 2 * REST, axis=1)[:, :REST])

    def weigh(n):
        def use(lo, value):
            width = value.shape[1]
            for at in range(0, width, 128):
                w = min(128, width - at)
                mixed = (
                    value[:TOK, at:at + w] * coef[0, :, :w] + value[TOK:, at:at + w] * coef[1, :, :w]
                )
                part[n, :, lo + at:lo + at + w] = mixed.astype(BF16)
        return use

    def keep(lo, value):
        raw[:, lo:lo + value.shape[1]] = value

    products(0, keep)

    for d in (1, 2, 3):
        to_x(stat, t_s, t_r, d).wait()
    top = prior
    for xx in range(NX):
        top = jnp.maximum(top, stat[xx, 0:1, :])
    whole = jnp.exp(prior - top)
    logit = jnp.zeros((1, TOK), F32)
    for xx in range(NX):
        whole += stat[xx, 1:2, :] * jnp.exp(stat[xx, 0:1, :] - top)
        logit += stat[xx, 2:3, :]
    lse = top + jnp.log(whole)
    weights = jnp.concatenate(
        [jnp.exp(peak - lse), jnp.where(owned, jnp.exp(my_target - lse) - 1.0, 0.0),
         jnp.zeros((6, TOK), F32)], axis=0,
    ).T
    coef[0] = jnp.broadcast_to(weights[:, 0:1], (TOK, 128))
    coef[1] = jnp.broadcast_to(weights[:, 1:2], (TOK, 128))

    def x_rows(d):
        return pl.ds(pl.multiple_of((x + d) % NX * SET, SET), SET)

    def x_half(d, way):
        return pl.ds(pl.multiple_of((x + d) % NX * SET + way * SUB, SUB), SUB)

    ways = ((0, 1, 3), (1, 3, 1))
    last = NK - 1

    def opposite_copy(n, way, d):
        return copy(part.at[n, x_half(2, way)], r1.at[n, way], o_s.at[n, way], o_r.at[n, way], x_dev(d))

    def direct_copy(n, way, d):
        return copy(part.at[n, x_half(d, way)], rd.at[n, way], d_s.at[n, way], d_r.at[n, way], x_dev(d))

    def sum_copy(n, way, d):
        return copy(s2.at[n, way], rs.at[n, way], q_s.at[n, way], q_r.at[n, way], x_dev(d))

    def straight_copy(d):
        return copy(part.at[last, x_rows(d)], r3.at[d - 1], w_s.at[d - 1], w_r.at[d - 1], x_dev(d))

    def z_copy(n):
        return copy(zs.at[n], zr.at[n], z_s.at[n], z_r.at[n], k_dev(quarters[n]))

    def send_first(n):
        if n == last:
            for d in (2, 1, 3):
                straight_copy(d).start()
            return
        for way, near, _ in ways:
            opposite_copy(n, way, near).start()
        for way, _, far in ways:
            direct_copy(n, way, far).start()

    def add_first(n):
        for way, near, _ in ways:
            opposite_copy(n, way, near).wait()
            s2[n, way] = (part[n, x_half(near, way), :].astype(F32) + r1[n, way].astype(F32)).astype(BF16)
            sum_copy(n, way, near).start()

    def add_last(n):
        for way, near, far in ways:
            direct_copy(n, way, far).wait()
            sum_copy(n, way, near).wait()
            zs[n, way * SUB:(way + 1) * SUB, :] = (
                part[n, x_half(0, way), :].astype(F32) + rd[n, way].astype(F32) + rs[n, way].astype(F32)
            ).astype(BF16)
        z_copy(n).start()

    for lo in range(0, QUARTER, 128):
        w = min(128, QUARTER - lo)
        part[0, :, lo:lo + w] = (
            raw[:TOK, lo:lo + w] * coef[0, :, :w] + raw[TOK:, lo:lo + w] * coef[1, :, :w]
        ).astype(BF16)
    send_first(0)
    lbuf[k] = jnp.broadcast_to(lse - logit, (8, TOK))

    def loss_to(d):
        return copy(lbuf.at[k], lbuf.at[k], l_s.at[d - 1], l_r.at[d - 1], k_dev((k + d) % NK))

    for d in (1, 2, 3):
        loss_to(d).start()
    products(1, weigh(1))
    send_first(1)
    add_first(0)
    products(2, weigh(2))
    send_first(2)
    add_first(1)
    products(3, weigh(3))
    send_first(3)
    add_first(2)
    add_last(0)
    add_last(1)

    for d in (1, 2, 3):
        loss_to(d).wait()
    result = jnp.zeros((8, TOK), F32)
    for kk in range(NK):
        turned = pltpu.roll(lbuf[kk], (kk + NX - x) % NX * SET, axis=1)
        result = jnp.where(lane_set == kk, turned, result)
    loss[...] = result[0:1]

    add_last(2)
    for n in range(2):
        z_copy(n).wait()
        out[set_rows((k + (2, 3)[n]) % NK), :] = zr[n]
    for d in (1, 2, 3):
        straight_copy(d).wait()
    value = part[last, x_rows(0), :].astype(F32)
    for d in (1, 2, 3):
        value += r3[d - 1].astype(F32)
    out[set_rows(k), :] = value.astype(BF16)
    z_copy(2).wait()
    out[set_rows((k + 1) % NK), :] = zr[2]


def body(hidden_states, embedding, targets, prior_lse):
    dma = pltpu.SemaphoreType.DMA
    vmem = pl.BlockSpec(memory_space=pltpu.VMEM)
    loss, grad = pl.pallas_call(
        kernel,
        out_shape=(
            jax.ShapeDtypeStruct((1, TOK), F32),
            jax.ShapeDtypeStruct((TOK, QUARTER), BF16),
        ),
        in_specs=[vmem] * 4,
        out_specs=(vmem, vmem),
        scratch_shapes=[
            pltpu.VMEM((ROWS, D), BF16),
            pltpu.VMEM((8, D), BF16),
            pltpu.VMEM((TOK, QUARTER), BF16),
            pltpu.VMEM((NX, NK, SET, QUARTER), BF16),
            pltpu.VMEM((TOK, D), BF16),
            pltpu.VMEM((2, ROWS, TOK), F32),
            pltpu.VMEM((2 * TOK, ROWS), BF16),
            pltpu.VMEM((2 * TOK, QUARTER), F32),
            pltpu.VMEM((2, TOK, 128), F32),
            pltpu.VMEM((NX, 8, TOK), F32),
            pltpu.VMEM((NX, 8, TOK), F32),
            pltpu.VMEM((NK, 8, TOK), F32),
            pltpu.VMEM((NK, TOK, QUARTER), BF16),
            pltpu.VMEM((NK - 1, 2, SUB, QUARTER), BF16),
            pltpu.VMEM((NK - 1, 2, SUB, QUARTER), BF16),
            pltpu.VMEM((NK - 1, 2, SUB, QUARTER), BF16),
            pltpu.VMEM((NK - 1, 2, SUB, QUARTER), BF16),
            pltpu.VMEM((NX - 1, SET, QUARTER), BF16),
            pltpu.VMEM((NK - 1, SET, QUARTER), BF16),
            pltpu.VMEM((NK - 1, SET, QUARTER), BF16),
            dma((2,)), dma((64,)), dma((64,)), dma((1,)), dma((1,)),
            dma((3,)), dma((3,)), dma((3, 4)), dma((3, 4)),
            dma((3,)), dma((3,)), dma((3,)), dma((3,)), dma((3,)), dma((3,)),
            dma((3, 2)), dma((3, 2)), dma((3, 2)), dma((3, 2)), dma((3, 2)), dma((3, 2)),
            dma((3,)), dma((3,)), dma((3,)), dma((3,)),
        ],
        compiler_params=pltpu.CompilerParams(
            collective_id=0, has_side_effects=True, vmem_limit_bytes=48 << 20
        ),
        cost_estimate=pl.CostEstimate(
            flops=6 * TOK * ROWS * D, bytes_accessed=4 * TOK * D, transcendentals=TOK * ROWS
        ),
    )(hidden_states.T, embedding, targets.reshape(1, TOK), prior_lse.reshape(1, TOK))
    return loss.reshape(TOK), grad


def solution(mesh):
    placed = (P("dp", "tensor"), P(("dp", "tensor"), None), P("dp"), P("dp"))
    return jax.shard_map(
        body, mesh=mesh, in_specs=placed, out_specs=(P("dp"), P("dp", "tensor")), check_vma=False
    )
```

time: 372 us -> 91.5 us (0.25)
  waiting for transfers between devices: 320 us -> 0 us
  Pallas kernels: 0 us -> 85.1 us
  blocking collectives: 18.6 us -> 0 us
  matrix products: 17.9 us -> 0 us
  between operations: 13.8 us -> 0.66 us
  local copies, waits for them, and re-layouts: 0.01 us -> 3.94 us
    all_gather x2 -> x0, waiting for transfers between devices: 275 us -> none  [the longest x1 225 us: body(): gathered = lax.all_gather(embedding, 'dp', axis=0, tiled=True)]
    pallas_call x0 -> x1, Pallas kernels: none -> 85.1 us  [body(): pl.pallas_call(kernel, out_shape=(jax.ShapeDtypeStruct((1, TOK), F32), ja...]
    reduce_scatter x1 -> x0, waiting for transfers between devices: 43.3 us -> none  [body(): lax.psum_scatter(partial_value.astype(jnp.bfloat16), 'tensor', scatter_di...]
    dot_general x2 -> x0, matrix products: 17.9 us -> none  [the longest x1 9.65 us: body(): jnp.dot(grad_logits, gathered, preferred_element_type=jnp.float32)]
    pmax x1 -> x0, blocking collectives: 11.3 us -> none  [body(): all_peak = lax.pmax(row_peak, 'tensor')]
    psum x1 -> x0, blocking collectives: 7.32 us -> none  [body(): lax.psum((row_total * jnp.exp(row_peak - all_peak), row_target), 'tensor')]
    unnamed x2 -> x10, local copies, waits for them, and re-layouts: 0.01 us -> 3.94 us
  transfers between devices with their start and end apart: 3 -> 0, of which waited for: 3 -> 0; matrix products, arithmetic and copies ran while one was open for 0% -> 0% of each run, Pallas kernels for 0% -> 0%
where the time goes in v2:
time: 91.5 us; the launch traced here: 89.7 us
  Pallas kernels  85.1 us (93%)
  local copies, waits for them, and re-layouts  3.94 us (4%)
    pallas_call x1, Pallas kernels, body(): pl.pallas_call(kernel, out_shape=(jax.ShapeDtypeStruct((1, TOK), F32), ja...  85.1 us
    unnamed x10, local copies, waits for them, and re-layouts  3.94 us

profile of v2, /device:TPU:1, one launch (start us, length us, event | category | flops | bytes accessed | tf_op | source)
XLA Modules:
  0.0 89.7 jit_solution(18138318820698795278)
XLA Ops:
  0.6 0.0 copy-start.2
  0.6 0.0 copy-start.3
  0.7 0.6 copy-done.2
  1.3 0.0 copy-done.3
  1.3 0.0 copy-start
  1.3 1.0 %copy-done = bf16[128,1344]{0,1:T(8,128)(2,1)S(1)} copy-done((bf16[128,1344]{0,1:T(8,128)(2,1)S(1)}, bf16[128,1344]{0,1:T(8,128)(2,1)}, u32[]{:S(2)}) %copy-start) | copy-done | bytes 344088
  2.3 0.0 copy-start.1
  2.3 0.9 copy-done.1
  3.2 85.1 %shard_map.59 = (f32[1,128]{1,0:T(1,128)S(1)}, bf16[128,1344]{1,0:T(8,128)(2,1)S(1)}) custom-call(bf16[1344,128]{1,0:T(8,128)(2,1)S(1)} %bitcast.4, bf16[8,5376]{1,0:T(8,128)(2,1)S(1)} %copy-done.1, s32[1,128]{1,0:T(1,128)S(1)} %bitcast.5, f32[1,128]{1,0:T(1,128)S(1)} %bitcast.6), custom_call_target="tpu_custom_call" | custom-call | flops 4227858432 | bytes 2752512 | tf_op jit(solution)/shard_map/pallas_call | solution.py:466
  88.3 0.9 %copy.6 = bf16[128,1344]{0,1:T(8,128)(2,1)} copy(bf16[128,1344]{1,0:T(8,128)(2,1)S(1)} %get-tuple-element.7) | data formatting | bytes 688128
  89.2 0.5 copy.8
Async XLA Ops:
  0.6 0.7 copy-start.2
  0.6 0.7 copy-start.3
  1.3 1.0 %copy-start = (bf16[128,1344]{0,1:T(8,128)(2,1)S(1)}, bf16[128,1344]{0,1:T(8,128)(2,1)}, u32[]{:S(2)}) copy-start(bf16[128,1344]{0,1:T(8,128)(2,1)} %param.4) | copy-start | bytes 1032196
  2.3 0.9 copy-start.1

commit v3 on v2

v3 whole, which is shorter than its diff:
```python
import functools

import jax
import jax.numpy as jnp
from jax import lax
from jax.experimental import pallas as pl
from jax.experimental.pallas import tpu as pltpu
from jax.sharding import PartitionSpec as P

MESH = pl.DeviceIdType.MESH
BF16 = jnp.bfloat16
F32 = jnp.float32
NX, NY, NZ, NK = 4, 8, 8, 4
D = 5376
QUARTER = D // NK
MAIN = QUARTER // 128 * 128
REST = QUARTER - MAIN
PART_A = 768
WIDTHS = (PART_A, QUARTER - PART_A)
KEPT = 3
SPLIT = 19 * 128
TOK = 128
SET = TOK // NK
SUB = SET // 2
PIECE = 16
BLOCK = 8 * PIECE
ROWS = NY * NZ * PIECE


def device(x, y, z, c):
    return (((z % 2) * NX + x) * NY + y) * 2 + c, z // 2


def at_row(row):
    return pl.ds(pl.multiple_of(row * PIECE, PIECE), PIECE)


def ring_offset(m):
    return ((m + 1) // 2) * (1 - 2 * (m % 2))


def rearranged(quarters):
    return jnp.concatenate(
        [q[:, :MAIN] for q in quarters] + [q[:, MAIN:] for q in quarters], axis=1
    )


def kernel(
    hid_hbm, emb_hbm, tgt_hbm, pri_hbm, loss, out,
    hid, emb, tgt, pri, g, ebuf, hidn, hb, ht, lt, gl, raw, coef, meta, stat, lbuf,
    part_a, part_b, r1_a, r1_b, s2_a, s2_b, rd_a, rd_b, r3_a, r3_b, zs_a, zs_b, zr_a, zr_b,
    in_s, e_s, g_r, s_r, g_s, s_s, ha_s, ha_r, hx_s, hx_r,
    m_s, m_r, t_s, t_r, l_s, l_r, o_s, o_r, d_s, d_r, q_s, w_s, w_r, z_s, z_r,
):
    dp = lax.axis_index("dp")
    k = lax.axis_index("tensor")
    c = dp % 2
    y = dp // 2 % NY
    x = dp // (2 * NY) % NX
    zl = dp // (2 * NY * NX)
    z = 2 * k + zl

    def x_dev(d):
        return device((x + d) % NX, y, z, c)

    def k_dev(kk):
        return device(x, y, 2 * kk + zl, c)

    sibling = device(x, y, z, 1 - c)

    arguments = [
        pltpu.make_async_copy(src, dst, in_s.at[n])
        for n, (src, dst) in enumerate(((hid_hbm, hid), (emb_hbm, emb), (tgt_hbm, tgt), (pri_hbm, pri)))
    ]
    for argument in arguments:
        argument.start()

    partners = [sibling]
    partners += [device(x, (y + d) % NY, z, c) for d in (1, 2, 6, 7)]
    partners += [device(x, y, (z + d) % NZ, c) for d in (1, 2, 4, 6, 7)]
    partners += [x_dev(d) for d in (1, 2, 3)]
    barrier = pltpu.get_barrier_semaphore()
    for partner in partners:
        pl.semaphore_signal(barrier, inc=1, device_id=partner, device_id_type=MESH)

    for argument in arguments:
        argument.wait()
    for lo in range(0, QUARTER, 128):
        hi = min(lo + 128, QUARTER)
        hidn[:, lo:hi] = hid[lo:hi, :].astype(F32).T.astype(BF16)
    t = tgt[...]
    b = t // 8
    t_dp, t_k = b // 4, b % 4
    t_z = 2 * t_k + t_dp // (2 * NY * NX)
    place = (t_dp // (2 * NY) % NX) * ROWS + (t_z * NY + t_dp // 2 % NY) * PIECE + t_dp % 2 * 8 + t % 8
    meta[x] = jnp.concatenate([place.astype(F32), pri[...], jnp.zeros((6, TOK), F32)], axis=0)
    pl.semaphore_wait(barrier, len(partners))

    def received(ref, recv):
        copy(ref, ref, e_s.at[0], recv, sibling).wait_recv()

    def sent(ref, send):
        copy(ref, ref, send, e_s.at[1], sibling).wait_send()

    def copy(src, dst, send, recv, where):
        return pltpu.make_async_remote_copy(
            src_ref=src, dst_ref=dst, send_sem=send, recv_sem=recv,
            device_id=where, device_id_type=MESH,
        )

    e_copy = copy(emb, ebuf, e_s.at[0], e_s.at[1], sibling)
    e_copy.start()

    def set_rows(kk):
        return pl.ds(pl.multiple_of(kk * SET, SET), SET)

    def hidden_set(d):
        kk = (k + d) % NK
        return copy(hidn.at[set_rows(kk)], hb.at[x, k], ha_s.at[0], ha_r.at[d - 1], k_dev(kk))

    def hidden_x(j, d):
        ref = hb.at[x, j]
        return copy(ref, ref, hx_s.at[0], hx_r.at[0], x_dev(d))

    def hidden_on(d):
        received(hb.at[x, (k + NK - d) % NK], ha_r.at[d - 1])
        for e in (1, 3, 2):
            hidden_x((k + NK - d) % NK, e).start()

    def to_x(buf, send, recv, d):
        return copy(buf.at[x], buf.at[x], send.at[0], recv.at[0], x_dev(d))

    hb[x, k] = hidn[set_rows(k), :]
    e_copy.wait()
    mine, other = emb[...], ebuf[...]
    rows = jnp.concatenate(
        [jnp.where(c == 0, mine, other), jnp.where(c == 0, other, mine)], axis=0
    )
    g[at_row(z * NY + y), :] = rearranged(
        [rows[:, j * QUARTER:(j + 1) * QUARTER] for j in range(NK)]
    )

    def bring_in(h):
        outer, inner = (z, y) if h == 0 else (y, z)
        spans = (slice(0, SPLIT), slice(SPLIT, D))

        def number(o, i):
            return o * 8 + i if h == 0 else i * 8 + o

        def ring_dev(o, i):
            return device(x, i, o, c) if h == 0 else device(x, o, i, c)

        outer_next = ring_dev((outer + 1) % 8, inner)
        outer_last = ring_dev((outer + 7) % 8, inner)

        def piece(n, share):
            return g.at[at_row(n), spans[share]]

        def to_ring(o, i, where, recv):
            ref = piece(number(o, i), h)
            copy(ref, ref, g_s.at[0], g_r.at[recv], where).start()

        def to_inner(i, d, recv):
            to_ring(outer, i, ring_dev(outer, (inner + d + 8) % 8), recv)

        def to_sibling(o, i):
            ref = piece(number(o, i), h)
            copy(ref, ref, s_s.at[0], s_r.at[o], sibling).start()

        def to_outer(m):
            i = (inner + ring_offset(m) + 8) % 8
            to_ring(outer, i, outer_next, 8 + m)
            to_ring(outer, i, outer_last, 8 + m)

        for m, d in ((1, 1), (2, -1), (3, 2), (4, -2)):
            to_inner(inner, d, m)
        to_outer(0)
        for e in (1, 3, 2):
            hidden_x(k, e).start()
        for d in (1, 2, 3):
            to_x(meta, m_s, m_r, d).start()

        def first(m, onward):
            i = (inner + ring_offset(m) + 8) % 8
            received(piece(number(outer, i), h), g_r.at[m])
            for to, d in onward:
                to_inner(i, d, to)
            to_outer(m)
            to_sibling(outer, i)

        def second(ring, start, end):
            up, down = (outer + 8 - ring) % 8, (outer + ring) % 8

            def step(m, carry):
                i = (inner + ring_offset(m) + 8) % 8
                received(g.at[0:2 * PIECE, spans[h]], g_r.at[ring * 8 + m])
                to = (ring + 1) * 8 + m
                if ring == 3:
                    pl.when(m % 2 == 1)(lambda: to_ring(up, i, outer_next, to))
                    pl.when(m % 2 == 0)(lambda: to_ring(down, i, outer_last, to))
                else:
                    to_ring(up, i, outer_next, to)
                    to_ring(down, i, outer_last, to)
                to_sibling(up, i)
                to_sibling(down, i)
                return carry

            lax.fori_loop(start, end, step, 0)

        def logits(share, offsets):
            o0 = outer if share == h else inner
            by_z = share == 0
            starts = []
            for r in offsets:
                o = (o0 + r) % 8
                if by_z:
                    starts.append((pl.multiple_of(o * BLOCK, BLOCK), BLOCK))
                else:
                    starts += [(pl.multiple_of((i * 8 + o) * PIECE, PIECE), PIECE) for i in range(8)]
            left = jnp.concatenate([g[pl.ds(a, n), spans[share]] for a, n in starts], axis=0)
            value = lax.dot_general(
                left, ht[:, spans[share]], (((1,), (1,)), ((), ())), preferred_element_type=F32
            )
            at = 0
            for a, n in starts:
                lt[share, pl.ds(a, n), :] = value[at:at + n]
                at += n

        def await_sibling(r):
            rows = BLOCK - PIECE if isinstance(r, int) and r == 0 else BLOCK
            received(g.at[0:rows, spans[1 - h]], s_r.at[(inner + r) % 8])

        def schedule():
            for m, onward in ((1, ()), (2, ()), (3, ((5, 1), (7, 2))), (4, ((6, -1),))):
                first(m, onward)
            for d in (1, 3, 2):
                hidden_set(d).start()
            second(1, 0, 5)
            for m in (5, 6, 7):
                first(m, ())
            second(2, 0, 5)
            hidden_on(1)
            hidden_on(3)
            second(1, 5, 8)
            hidden_on(2)
            second(2, 5, 8)

        schedule()
        received(hb.at[0:NX - 1], hx_r.at[0])
        for xx in range(NX):
            ht[xx * SET:(xx + 1) * SET, :] = rearranged([hb[xx, j] for j in range(NK)])

        def early(r, carry):
            second(3, 4 * (r - 1), 4 * r)
            logits(h, (r, 8 - r))
            await_sibling(r)
            await_sibling(8 - r)
            logits(1 - h, (r, 8 - r))
            return carry

        lax.fori_loop(1, 3, early, 0)
        logits(h, (3, 5))
        logits(h, (0,))
        await_sibling(0)
        logits(1 - h, (0,))
        await_sibling(3)
        await_sibling(5)
        logits(1 - h, (3, 5))
        across = (outer + 4) % 8
        for m in range(8):
            i = (inner + ring_offset(m) + 8) % 8
            received(piece(number(across, i), h), g_r.at[32 + m])
            to_sibling(across, i)
        logits(h, (4,))
        await_sibling(4)
        logits(1 - h, (4,))

        sent(g.at[0:ROWS - PIECE, spans[h]], g_s.at[0])
        sent(g.at[0:ROWS - PIECE, spans[h]], s_s.at[0])

    for core in (0, 1):
        pl.when(c == core)(functools.partial(bring_in, core))

    lane_set = lax.broadcasted_iota(jnp.int32, (8, TOK), 1) // SET
    received(meta.at[0:NX - 1], m_r.at[0])
    info = jnp.zeros((8, TOK), F32)
    for xx in range(NX):
        turned = pltpu.roll(meta[xx], (xx + NX - k) % NX * SET, axis=1)
        info = jnp.where(lane_set == xx, turned, info)
    column = info[0:1] - (x * ROWS).astype(F32)
    owned = (column >= 0.0) & (column < float(ROWS))
    prior = info[1:2]

    peaks = jnp.full((8, TOK), -jnp.inf, F32)
    for n in range(8):
        span = slice(n * BLOCK, (n + 1) * BLOCK)
        value = lt[0, span, :] + lt[1, span, :]
        lt[0, span, :] = value
        peaks = jnp.maximum(peaks, jnp.max(value.reshape(BLOCK // 8, 8, TOK), axis=0))
    peak = jnp.max(peaks, axis=0, keepdims=True)
    total = jnp.zeros((8, TOK), F32)
    target = jnp.zeros((8, TOK), F32)
    row_id = lax.broadcasted_iota(jnp.int32, (BLOCK, TOK), 0).astype(F32)
    for n in range(8):
        span = slice(n * BLOCK, (n + 1) * BLOCK)
        value = lt[0, span, :]
        hit = row_id == column - float(n * BLOCK)
        power = jnp.exp(value - peak)
        lt[1, span, :] = jnp.where(hit, 0.0, power)
        total += jnp.sum(power.reshape(BLOCK // 8, 8, TOK), axis=0)
        target += jnp.sum(jnp.where(hit, value, 0.0).reshape(BLOCK // 8, 8, TOK), axis=0)
    my_target = jnp.sum(target, axis=0, keepdims=True)
    stat[x] = jnp.concatenate(
        [peak, jnp.sum(total, axis=0, keepdims=True), my_target, jnp.zeros((5, TOK), F32)], axis=0
    )
    for d in (1, 2, 3):
        to_x(stat, t_s, t_r, d).start()

    column_t = jnp.broadcast_to(column, (8, TOK)).T[:, 0:1]
    lane_id = lax.broadcasted_iota(jnp.int32, (TOK, BLOCK), 1).astype(F32)
    for n in range(8):
        span = slice(n * BLOCK, (n + 1) * BLOCK)
        gl[0:TOK, span] = lt[1, span, :].T.astype(BF16)
        gl[TOK:, span] = jnp.where(lane_id == column_t - float(n * BLOCK), 1.0, 0.0).astype(BF16)

    units = ((2, 1), (2, 0), (1, 0), (3, 0), (1, 1), (3, 1), (0, 0), (0, 1))
    turns = (2, 1, 3, 0)
    parts, r1s, s2s, rds = (part_a, part_b), (r1_a, r1_b), (s2_a, s2_b), (rd_a, rd_b)
    r3s, zss, zrs = (r3_a, r3_b), (zs_a, zs_b), (zr_a, zr_b)

    def place_of(u):
        turn, p = units[u]
        return turns.index(turn), p

    def products(u, use):
        turn, p = units[u]
        j = (k + turn) % NK
        for lo, hi in ((0, 512), (512, PART_A)) if p == 0 else ((PART_A, MAIN),):
            at = pl.ds(pl.multiple_of(j * MAIN + lo, 128), hi - lo)
            use(lo - p * PART_A, jnp.dot(gl[...], g[:, at], preferred_element_type=F32))
        if p == 1:
            at = pl.ds(pl.multiple_of(NK * MAIN + j // 2 * 128, 128), 128)
            value = jnp.dot(gl[...], g[:, at], preferred_element_type=F32)
            use(MAIN - PART_A, pltpu.roll(value, j % 2 * REST, axis=1)[:, :REST])

    def weigh(u):
        q, p = place_of(u)

        def use(lo, value):
            for at in range(0, value.shape[1], 128):
                w = min(128, value.shape[1] - at)
                mixed = (
                    value[:TOK, at:at + w] * coef[0, :, :w] + value[TOK:, at:at + w] * coef[1, :, :w]
                )
                parts[p][q, :, lo + at:lo + at + w] = mixed.astype(BF16)

        return use

    def keep(u):
        def use(lo, value):
            raw[u, :, lo:lo + value.shape[1]] = value

        return use

    for u in range(KEPT):
        products(u, keep(u))

    received(stat.at[0:NX - 1], t_r.at[0])
    top = prior
    for xx in range(NX):
        top = jnp.maximum(top, stat[xx, 0:1, :])
    whole = jnp.exp(prior - top)
    logit = jnp.zeros((1, TOK), F32)
    for xx in range(NX):
        whole += stat[xx, 1:2, :] * jnp.exp(stat[xx, 0:1, :] - top)
        logit += stat[xx, 2:3, :]
    lse = top + jnp.log(whole)
    weights = jnp.concatenate(
        [jnp.exp(peak - lse), jnp.where(owned, jnp.exp(my_target - lse) - 1.0, 0.0),
         jnp.zeros((6, TOK), F32)], axis=0,
    ).T
    coef[0] = jnp.broadcast_to(weights[:, 0:1], (TOK, 128))
    coef[1] = jnp.broadcast_to(weights[:, 1:2], (TOK, 128))

    def x_rows(d):
        return pl.ds(pl.multiple_of((x + d) % NX * SET, SET), SET)

    def x_half(d, way):
        return pl.ds(pl.multiple_of((x + d) % NX * SET + way * SUB, SUB), SUB)

    ways = ((0, 1, 3), (1, 3, 1))

    def opposite_copy(u, way, d):
        q, p = place_of(u)
        return copy(parts[p].at[q, x_half(2, way)], r1s[p].at[q, way], o_s.at[p], o_r.at[u], x_dev(d))

    def direct_copy(u, way, d):
        q, p = place_of(u)
        return copy(parts[p].at[q, x_half(d, way)], rds[p].at[q, way], d_s.at[p], d_r.at[u], x_dev(d))

    def sum_copy(u, way, d):
        q, p = place_of(u)
        return copy(s2s[p].at[q, way], rds[p].at[q, 2 + way], q_s.at[p], d_r.at[u], x_dev(d))

    def straight_copy(p, d):
        return copy(parts[p].at[3, x_rows(d)], r3s[p].at[d - 1], w_s.at[p], w_r.at[p], x_dev(d))

    def z_copy(u):
        q, p = place_of(u)
        return copy(zss[p].at[q], zrs[p].at[q], z_s.at[p], z_r.at[u], k_dev((k + units[u][0]) % NK))

    def send_first(u):
        q, p = place_of(u)
        if q == 3:
            for d in (2, 1, 3):
                straight_copy(p, d).start()
            return
        for way, near, _ in ways:
            opposite_copy(u, way, near).start()
        for way, _, far in ways:
            direct_copy(u, way, far).start()

    def multiply(u):
        if u < KEPT:
            width = WIDTHS[units[u][1]]
            for lo in range(0, width, 128):
                weigh(u)(lo, raw[u, :, lo:min(lo + 128, width)])
        else:
            products(u, weigh(u))
        send_first(u)

    def add_first(u):
        q, p = place_of(u)
        received(r1s[p].at[q], o_r.at[u])
        for way, near, _ in ways:
            s2s[p][q, way] = (
                parts[p][q, x_half(near, way), :].astype(F32) + r1s[p][q, way].astype(F32)
            ).astype(BF16)
            sum_copy(u, way, near).start()

    def add_last(u):
        q, p = place_of(u)
        received(rds[p].at[q], d_r.at[u])
        for way in (0, 1):
            zss[p][q, way * SUB:(way + 1) * SUB, :] = (
                parts[p][q, x_half(0, way), :].astype(F32)
                + rds[p][q, way].astype(F32) + rds[p][q, 2 + way].astype(F32)
            ).astype(BF16)
        z_copy(u).start()

    def own(p):
        received(r3s[p], w_r.at[p])
        value = parts[p][3, x_rows(0), :].astype(F32)
        for d in (1, 2, 3):
            value += r3s[p][d - 1].astype(F32)
        out[set_rows(k), p * PART_A:p * PART_A + WIDTHS[p]] = value.astype(BF16)

    def finish(u):
        q, p = place_of(u)
        received(zrs[p].at[q], z_r.at[u])
        rows = set_rows((k + NK - units[u][0]) % NK)
        out[rows, p * PART_A:p * PART_A + WIDTHS[p]] = zrs[p][q]

    multiply(0)
    lbuf[k] = jnp.broadcast_to(lse - logit, (8, TOK))

    def loss_to(d):
        return copy(lbuf.at[k], lbuf.at[k], l_s.at[0], l_r.at[0], k_dev((k + d) % NK))

    for d in (1, 2, 3):
        loss_to(d).start()
    multiply(1)
    multiply(2)
    multiply(3)
    add_first(0)
    multiply(4)
    add_first(1)
    multiply(5)
    add_first(2)
    add_first(3)
    add_last(0)
    add_first(4)
    add_last(1)
    add_first(5)
    multiply(6)
    add_last(2)
    multiply(7)
    add_last(3)
    add_last(4)
    add_last(5)

    received(lbuf.at[0:NK - 1], l_r.at[0])
    result = jnp.zeros((8, TOK), F32)
    for kk in range(NK):
        turned = pltpu.roll(lbuf[kk], (kk + NX - x) % NX * SET, axis=1)
        result = jnp.where(lane_set == kk, turned, result)
    loss[...] = result[0:1]

    finish(0)
    finish(1)
    own(0)
    own(1)
    for u in (2, 4, 3, 5):
        finish(u)

    sent(hidn.at[0:TOK - SET], ha_s.at[0])
    sent(hb.at[0:NX - 1], hx_s.at[0])
    for buf, send in ((meta, m_s), (stat, t_s), (lbuf, l_s)):
        sent(buf.at[0:3], send.at[0])
    for p in (0, 1):
        sent(r1s[p], o_s.at[p])
        sent(r1s[p], d_s.at[p])
        sent(r1s[p], q_s.at[p])
        sent(r3s[p], w_s.at[p])
        sent(zss[p], z_s.at[p])


def body(hidden_states, embedding, targets, prior_lse):
    dma = pltpu.SemaphoreType.DMA
    hbm = pl.BlockSpec(memory_space=pltpu.HBM)
    vmem = pl.BlockSpec(memory_space=pltpu.VMEM)
    arguments = (hidden_states.T, embedding, targets.reshape(1, TOK), prior_lse.reshape(1, TOK))
    pair = [(WIDTHS[0],), (WIDTHS[1],)]
    loss, grad = pl.pallas_call(
        kernel,
        out_shape=(
            jax.ShapeDtypeStruct((1, TOK), F32),
            jax.ShapeDtypeStruct((TOK, QUARTER), BF16),
        ),
        in_specs=[hbm] * 4,
        out_specs=(vmem, vmem),
        scratch_shapes=[
            pltpu.VMEM((QUARTER, TOK), BF16),
            pltpu.VMEM((8, D), BF16),
            pltpu.VMEM((1, TOK), jnp.int32),
            pltpu.VMEM((1, TOK), F32),
            pltpu.VMEM((ROWS, D), BF16),
            pltpu.VMEM((8, D), BF16),
            pltpu.VMEM((TOK, QUARTER), BF16),
            pltpu.VMEM((NX, NK, SET, QUARTER), BF16),
            pltpu.VMEM((TOK, D), BF16),
            pltpu.VMEM((2, ROWS, TOK), F32),
            pltpu.VMEM((2 * TOK, ROWS), BF16),
            pltpu.VMEM((KEPT, 2 * TOK, WIDTHS[0]), F32),
            pltpu.VMEM((2, TOK, 128), F32),
            pltpu.VMEM((NX, 8, TOK), F32),
            pltpu.VMEM((NX, 8, TOK), F32),
            pltpu.VMEM((NK, 8, TOK), F32),
            *[pltpu.VMEM((NK, TOK) + w, BF16) for w in pair],
            *[pltpu.VMEM((NK - 1, 2, SUB) + w, BF16) for w in pair * 2],
            *[pltpu.VMEM((NK - 1, 4, SUB) + w, BF16) for w in pair],
            *[pltpu.VMEM((NX - 1, SET) + w, BF16) for w in pair],
            *[pltpu.VMEM((NK - 1, SET) + w, BF16) for w in pair * 2],
            *[dma((n,)) for n in (4, 2, 40, 8, 1, 1, 1, 3, 1, 1)],
            *[dma((n,)) for n in (1, 1, 1, 1, 1, 1, 2, 6, 2, 6, 2, 2, 2, 2, 6)],
        ],
        compiler_params=pltpu.CompilerParams(
            collective_id=0, has_side_effects=True, vmem_limit_bytes=48 << 20
        ),
        cost_estimate=pl.CostEstimate(
            flops=6 * TOK * ROWS * D, bytes_accessed=4 * TOK * D, transcendentals=TOK * ROWS
        ),
    )(*[pltpu.with_memory_space_constraint(a, pltpu.HBM) for a in arguments])
    return loss.reshape(TOK), grad


def solution(mesh):
    placed = (P("dp", "tensor"), P(("dp", "tensor"), None), P("dp"), P("dp"))
    return jax.shard_map(
        body, mesh=mesh, in_specs=placed, out_specs=(P("dp"), P("dp", "tensor")), check_vma=False
    )
```

time: 91.5 us -> 83.8 us (0.916); the launches traced: 89.7 us -> 83.6 us
  Pallas kernels: 85.1 us -> 81.6 us
  local copies, waits for them, and re-layouts: 3.94 us -> 1.42 us
    pallas_call x1, Pallas kernels: 85.1 us -> 81.6 us  [body(): pl.pallas_call(kernel, out_shape=(jax.ShapeDtypeStruct((1, TOK), F32), ja...]
    unnamed x10 -> x2, local copies, waits for them, and re-layouts: 3.94 us -> 1.42 us
where the time goes in v3:
time: 83.8 us; the launch traced here: 83.6 us
  Pallas kernels  81.6 us (97%)
  local copies, waits for them, and re-layouts  1.42 us (2%)
    pallas_call x1, Pallas kernels, body(): pl.pallas_call(kernel, out_shape=(jax.ShapeDtypeStruct((1, TOK), F32), ja...  81.6 us

profile of v3, /device:TPU:1, one launch (start us, length us, event | category | flops | bytes accessed | tf_op | source)
XLA Modules:
  0.0 83.6 jit_solution(4463159132891860797)
XLA Ops:
  0.6 81.6 %shard_map.59 = (f32[1,128]{1,0:T(1,128)S(1)}, bf16[128,1344]{1,0:T(8,128)(2,1)S(1)}) custom-call(bf16[1344,128]{1,0:T(8,128)(2,1)} %bitcast.5, bf16[8,5376]{1,0:T(8,128)(2,1)} %emb_hbm.1, s32[1,128]{1,0:T(1,128)} %bitcast.6, f32[1,128]{1,0:T(1,128)} %bitcast.7), custom_call_target="tpu_custom_call" | custom-call | flops 4227858432 | bytes 2752512 | tf_op jit(solution)/shard_map/pallas_call | solution.py:524
  82.2 0.9 %copy.6 = bf16[128,1344]{0,1:T(8,128)(2,1)} copy(bf16[128,1344]{1,0:T(8,128)(2,1)S(1)} %get-tuple-element.7) | data formatting | bytes 688128
  83.1 0.5 copy.8

commit v4 on v3

--- a/solution.py
+++ b/solution.py
@@ -27,6 +27,26 @@
 ROWS = NY * NZ * PIECE
 
 
+STEPS = (
+    (
+        ("send", 1), ("send", 3), ("send", 2), ("first", 1, 8, False), ("outer", 0), ("outer", 1),
+        ("outer", 2), ("outer", 3), ("outer", 4), ("outer", 5), ("outer", 6), ("outer", 7),
+        ("pass", 1), ("pass", 3), ("pass", 2), ("second", 1, 0, 8), ("second", 2, 0, 5),
+        ("features",), ("own", 0), ("sibling", 0), ("second", 2, 5, 8), ("own", 1),
+        ("second", 3, 0, 4), ("sibling", 1), ("own", 2), ("second", 3, 4, 8), ("sibling", 2),
+        ("own", 3), ("sibling", 3), ("opposite",), ("own", 4), ("sibling", 4),
+    ),
+    (
+        ("outer", 0), ("send", 1), ("send", 3), ("send", 2), ("first", 1, 5, True),
+        ("second", 1, 0, 5), ("first", 5, 8, True), ("pass", 1), ("pass", 3), ("pass", 2),
+        ("second", 2, 0, 5), ("second", 1, 5, 8), ("features",), ("own", 0), ("sibling", 0),
+        ("own", 1), ("second", 2, 5, 8), ("second", 3, 0, 4), ("sibling", 1), ("own", 2),
+        ("second", 3, 4, 8), ("sibling", 2), ("own", 3), ("sibling", 3), ("opposite",), ("own", 4),
+        ("sibling", 4),
+    ),
+)
+
+
 def device(x, y, z, c):
     return (((z % 2) * NX + x) * NY + y) * 2 + c, z // 2
 
@@ -174,19 +194,20 @@
 
         for m, d in ((1, 1), (2, -1), (3, 2), (4, -2)):
             to_inner(inner, d, m)
-        to_outer(0)
         for e in (1, 3, 2):
             hidden_x(k, e).start()
         for d in (1, 2, 3):
             to_x(meta, m_s, m_r, d).start()
 
-        def first(m, onward):
-            i = (inner + ring_offset(m) + 8) % 8
-            received(piece(number(outer, i), h), g_r.at[m])
-            for to, d in onward:
-                to_inner(i, d, to)
-            to_outer(m)
-            to_sibling(outer, i)
+        def first(start, end, outward):
+            for m in range(start, end):
+                i = (inner + ring_offset(m) + 8) % 8
+                received(piece(number(outer, i), h), g_r.at[m])
+                for to, d in {3: ((5, 1), (7, 2)), 4: ((6, -1),)}.get(m, ()):
+                    to_inner(i, d, to)
+                if outward:
+                    to_outer(m)
+                to_sibling(outer, i)
 
         def second(ring, start, end):
             up, down = (outer + 8 - ring) % 8, (outer + ring) % 8
@@ -230,50 +251,33 @@
             rows = BLOCK - PIECE if isinstance(r, int) and r == 0 else BLOCK
             received(g.at[0:rows, spans[1 - h]], s_r.at[(inner + r) % 8])
 
-        def schedule():
-            for m, onward in ((1, ()), (2, ()), (3, ((5, 1), (7, 2))), (4, ((6, -1),))):
-                first(m, onward)
-            for d in (1, 3, 2):
-                hidden_set(d).start()
-            second(1, 0, 5)
-            for m in (5, 6, 7):
-                first(m, ())
-            second(2, 0, 5)
-            hidden_on(1)
-            hidden_on(3)
-            second(1, 5, 8)
-            hidden_on(2)
-            second(2, 5, 8)
-
-        schedule()
-        received(hb.at[0:NX - 1], hx_r.at[0])
-        for xx in range(NX):
-            ht[xx * SET:(xx + 1) * SET, :] = rearranged([hb[xx, j] for j in range(NK)])
-
-        def early(r, carry):
-            second(3, 4 * (r - 1), 4 * r)
-            logits(h, (r, 8 - r))
-            await_sibling(r)
-            await_sibling(8 - r)
-            logits(1 - h, (r, 8 - r))
-            return carry
-
-        lax.fori_loop(1, 3, early, 0)
-        logits(h, (3, 5))
-        logits(h, (0,))
-        await_sibling(0)
-        logits(1 - h, (0,))
-        await_sibling(3)
-        await_sibling(5)
-        logits(1 - h, (3, 5))
-        across = (outer + 4) % 8
-        for m in range(8):
-            i = (inner + ring_offset(m) + 8) % 8
-            received(piece(number(across, i), h), g_r.at[32 + m])
-            to_sibling(across, i)
-        logits(h, (4,))
-        await_sibling(4)
-        logits(1 - h, (4,))
+        def features():
+            received(hb.at[0:NX - 1], hx_r.at[0])
+            for xx in range(NX):
+                ht[xx * SET:(xx + 1) * SET, :] = rearranged([hb[xx, j] for j in range(NK)])
+
+        def own_logits(r):
+            logits(h, (r,) if r % 4 == 0 else (r, 8 - r))
+
+        def sibling_logits(r):
+            for b in (r,) if r % 4 == 0 else (r, 8 - r):
+                await_sibling(b)
+            logits(1 - h, (r,) if r % 4 == 0 else (r, 8 - r))
+
+        def opposite():
+            across = (outer + 4) % 8
+            for m in range(8):
+                i = (inner + ring_offset(m) + 8) % 8
+                received(piece(number(across, i), h), g_r.at[32 + m])
+                to_sibling(across, i)
+
+        acts = {
+            "first": first, "outer": to_outer, "second": second, "opposite": opposite,
+            "send": lambda d: hidden_set(d).start(), "pass": hidden_on, "features": features,
+            "own": own_logits, "sibling": sibling_logits,
+        }
+        for act, *numbers in STEPS[h]:
+            acts[act](*numbers)
 
         sent(g.at[0:ROWS - PIECE, spans[h]], g_s.at[0])
         sent(g.at[0:ROWS - PIECE, spans[h]], s_s.at[0])
@@ -482,12 +486,12 @@
     add_first(4)
     add_last(1)
     add_first(5)
+    add_last(2)
+    add_last(3)
     multiply(6)
-    add_last(2)
-    multiply(7)
-    add_last(3)
     add_last(4)
     add_last(5)
+    multiply(7)
 
     received(lbuf.at[0:NK - 1], l_r.at[0])
     result = jnp.zeros((8, TOK), F32)

time: 83.8 us -> 81.4 us (0.971)
  Pallas kernels: 81.6 us -> 79.2 us
    pallas_call x1, Pallas kernels: 81.6 us -> 79.2 us  [body(): pl.pallas_call(kernel, out_shape=(jax.ShapeDtypeStruct((1, TOK), F32), ja...]
where the time goes in v4:
time: 81.4 us; the launch traced here: 81.3 us
  Pallas kernels  79.2 us (97%)
  local copies, waits for them, and re-layouts  1.42 us (2%)
    pallas_call x1, Pallas kernels, body(): pl.pallas_call(kernel, out_shape=(jax.ShapeDtypeStruct((1, TOK), F32), ja...  79.2 us

profile of v4, /device:TPU:1, one launch (start us, length us, event | category | flops | bytes accessed | tf_op | source)
XLA Modules:
  0.0 81.3 jit_solution(10452895533676277739)
XLA Ops:
  0.6 79.2 %shard_map.59 = (f32[1,128]{1,0:T(1,128)S(1)}, bf16[128,1344]{1,0:T(8,128)(2,1)S(1)}) custom-call(bf16[1344,128]{1,0:T(8,128)(2,1)} %bitcast.5, bf16[8,5376]{1,0:T(8,128)(2,1)} %emb_hbm.1, s32[1,128]{1,0:T(1,128)} %bitcast.6, f32[1,128]{1,0:T(1,128)} %bitcast.7), custom_call_target="tpu_custom_call" | custom-call | flops 4227858432 | bytes 2752512 | tf_op jit(solution)/shard_map/pallas_call | solution.py:528
  79.9 0.9 %copy.6 = bf16[128,1344]{0,1:T(8,128)(2,1)} copy(bf16[128,1344]{1,0:T(8,128)(2,1)S(1)} %get-tuple-element.7) | data formatting | bytes 688128
  80.8 0.5 copy.8

commit v5 on v4

--- a/solution.py
+++ b/solution.py
@@ -17,7 +17,7 @@
 REST = QUARTER - MAIN
 PART_A = 768
 WIDTHS = (PART_A, QUARTER - PART_A)
-KEPT = 3
+KEPT = 5
 SPLIT = 19 * 128
 TOK = 128
 SET = TOK // NK
@@ -29,20 +29,21 @@
 
 STEPS = (
     (
-        ("send", 1), ("send", 3), ("send", 2), ("first", 1, 8, False), ("outer", 0), ("outer", 1),
-        ("outer", 2), ("outer", 3), ("outer", 4), ("outer", 5), ("outer", 6), ("outer", 7),
-        ("pass", 1), ("pass", 3), ("pass", 2), ("second", 1, 0, 8), ("second", 2, 0, 5),
-        ("features",), ("own", 0), ("sibling", 0), ("second", 2, 5, 8), ("own", 1),
+        ("send", 1), ("send", 3), ("send", 2), ("first", 1, 3, False), ("outer", 0), ("outer", 1),
+        ("first", 3, 8, False), ("pass", 1), ("pass", 3), ("pass", 2), ("outer", 2), ("outer", 3),
+        ("outer", 4), ("second", 1, 0, 1), ("outer", 5), ("outer", 6), ("outer", 7),
+        ("second", 1, 1, 8), ("second", 2, 0, 5), ("features",), ("own", 0), ("sibling", 0),
+        ("second", 2, 5, 8), ("own", 1), ("second", 3, 0, 4), ("sibling", 1), ("own", 2),
+        ("second", 3, 4, 8), ("sibling", 2), ("own", 3), ("sibling", 3), ("opposite",), ("own", 4),
+        ("sibling", 4),
+    ),
+    (
+        ("outer", 0), ("send", 1), ("send", 3), ("send", 2), ("second", 1, 0, 1),
+        ("second", 2, 0, 1), ("first", 1, 5, True), ("pass", 1), ("pass", 3), ("pass", 2),
+        ("second", 1, 1, 5), ("first", 5, 8, True), ("second", 2, 1, 5), ("second", 1, 5, 8),
+        ("features",), ("own", 0), ("sibling", 0), ("own", 1), ("second", 2, 5, 8),
         ("second", 3, 0, 4), ("sibling", 1), ("own", 2), ("second", 3, 4, 8), ("sibling", 2),
         ("own", 3), ("sibling", 3), ("opposite",), ("own", 4), ("sibling", 4),
-    ),
-    (
-        ("outer", 0), ("send", 1), ("send", 3), ("send", 2), ("first", 1, 5, True),
-        ("second", 1, 0, 5), ("first", 5, 8, True), ("pass", 1), ("pass", 3), ("pass", 2),
-        ("second", 2, 0, 5), ("second", 1, 5, 8), ("features",), ("own", 0), ("sibling", 0),
-        ("own", 1), ("second", 2, 5, 8), ("second", 3, 0, 4), ("sibling", 1), ("own", 2),
-        ("second", 3, 4, 8), ("sibling", 2), ("own", 3), ("sibling", 3), ("opposite",), ("own", 4),
-        ("sibling", 4),
     ),
 )
 
@@ -425,12 +426,9 @@
             direct_copy(u, way, far).start()
 
     def multiply(u):
-        if u < KEPT:
-            width = WIDTHS[units[u][1]]
-            for lo in range(0, width, 128):
-                weigh(u)(lo, raw[u, :, lo:min(lo + 128, width)])
-        else:
-            products(u, weigh(u))
+        _, p = place_of(u)
+        for lo in range(0, WIDTHS[p], 128):
+            weigh(u)(lo, raw[u, :, lo:min(lo + 128, WIDTHS[p])])
         send_first(u)
 
     def add_first(u):
@@ -475,12 +473,14 @@
         loss_to(d).start()
     multiply(1)
     multiply(2)
+    for u in range(KEPT, 8):
+        products(u, keep(u))
+    add_first(0)
     multiply(3)
-    add_first(0)
+    add_first(1)
     multiply(4)
-    add_first(1)
+    add_first(2)
     multiply(5)
-    add_first(2)
     add_first(3)
     add_last(0)
     add_first(4)
@@ -490,8 +490,8 @@
     add_last(3)
     multiply(6)
     add_last(4)
+    multiply(7)
     add_last(5)
-    multiply(7)
 
     received(lbuf.at[0:NK - 1], l_r.at[0])
     result = jnp.zeros((8, TOK), F32)
@@ -545,7 +545,7 @@
             pltpu.VMEM((TOK, D), BF16),
             pltpu.VMEM((2, ROWS, TOK), F32),
             pltpu.VMEM((2 * TOK, ROWS), BF16),
-            pltpu.VMEM((KEPT, 2 * TOK, WIDTHS[0]), F32),
+            pltpu.VMEM((8, 2 * TOK, WIDTHS[0]), F32),
             pltpu.VMEM((2, TOK, 128), F32),
             pltpu.VMEM((NX, 8, TOK), F32),
             pltpu.VMEM((NX, 8, TOK), F32),

time: 81.4 us -> 79.9 us (0.982)
  Pallas kernels: 79.2 us -> 77.7 us
    pallas_call x1, Pallas kernels: 79.2 us -> 77.7 us  [body(): pl.pallas_call(kernel, out_shape=(jax.ShapeDtypeStruct((1, TOK), F32), ja...]
where the time goes in v5:
time: 79.9 us; the launch traced here: 79.8 us
  Pallas kernels  77.7 us (97%)
  local copies, waits for them, and re-layouts  1.42 us (2%)
    pallas_call x1, Pallas kernels, body(): pl.pallas_call(kernel, out_shape=(jax.ShapeDtypeStruct((1, TOK), F32), ja...  77.7 us

profile of v5, /device:TPU:1, one launch (start us, length us, event | category | flops | bytes accessed | tf_op | source)
XLA Modules:
  0.0 79.8 jit_solution(1153535664530495421)
XLA Ops:
  0.6 77.7 %shard_map.59 = (f32[1,128]{1,0:T(1,128)S(1)}, bf16[128,1344]{1,0:T(8,128)(2,1)S(1)}) custom-call(bf16[1344,128]{1,0:T(8,128)(2,1)} %bitcast.5, bf16[8,5376]{1,0:T(8,128)(2,1)} %emb_hbm.1, s32[1,128]{1,0:T(1,128)} %bitcast.6, f32[1,128]{1,0:T(1,128)} %bitcast.7), custom_call_target="tpu_custom_call" | custom-call | flops 4227858432 | bytes 2752512 | tf_op jit(solution)/shard_map/pallas_call | solution.py:528
  78.4 0.9 %copy.6 = bf16[128,1344]{0,1:T(8,128)(2,1)} copy(bf16[128,1344]{1,0:T(8,128)(2,1)S(1)} %get-tuple-element.7) | data formatting | bytes 688128
  79.3 0.5 copy.8

commit v6 on v5

--- a/solution.py
+++ b/solution.py
@@ -18,7 +18,7 @@
 PART_A = 768
 WIDTHS = (PART_A, QUARTER - PART_A)
 KEPT = 5
-SPLIT = 19 * 128
+SPLIT = 18 * 128
 TOK = 128
 SET = TOK // NK
 SUB = SET // 2
@@ -29,21 +29,20 @@
 
 STEPS = (
     (
-        ("send", 1), ("send", 3), ("send", 2), ("first", 1, 3, False), ("outer", 0), ("outer", 1),
-        ("first", 3, 8, False), ("pass", 1), ("pass", 3), ("pass", 2), ("outer", 2), ("outer", 3),
-        ("outer", 4), ("second", 1, 0, 1), ("outer", 5), ("outer", 6), ("outer", 7),
-        ("second", 1, 1, 8), ("second", 2, 0, 5), ("features",), ("own", 0), ("sibling", 0),
-        ("second", 2, 5, 8), ("own", 1), ("second", 3, 0, 4), ("sibling", 1), ("own", 2),
-        ("second", 3, 4, 8), ("sibling", 2), ("own", 3), ("sibling", 3), ("opposite",), ("own", 4),
-        ("sibling", 4),
+        ("first", 1, 3, False), ("send", 1), ("send", 3), ("send", 2), ("outer", 0), ("outer", 1),
+        ("first", 3, 8, False), ("outer", 2), ("outer", 3), ("outer", 4), ("pass", 1), ("pass", 3),
+        ("pass", 2), ("outer", 5), ("outer", 6), ("outer", 7), ("second", 1, 0, 8),
+        ("second", 2, 0, 5), ("features",), ("own", 0), ("sibling", 0), ("second", 2, 5, 8),
+        ("own", 1), ("second", 3, 0, 4), ("sibling", 1), ("own", 2), ("second", 3, 4, 8),
+        ("sibling", 2), ("own", 3), ("sibling", 3), ("opposite",), ("own", 4), ("sibling", 4),
     ),
     (
-        ("outer", 0), ("send", 1), ("send", 3), ("send", 2), ("second", 1, 0, 1),
-        ("second", 2, 0, 1), ("first", 1, 5, True), ("pass", 1), ("pass", 3), ("pass", 2),
-        ("second", 1, 1, 5), ("first", 5, 8, True), ("second", 2, 1, 5), ("second", 1, 5, 8),
-        ("features",), ("own", 0), ("sibling", 0), ("own", 1), ("second", 2, 5, 8),
-        ("second", 3, 0, 4), ("sibling", 1), ("own", 2), ("second", 3, 4, 8), ("sibling", 2),
-        ("own", 3), ("sibling", 3), ("opposite",), ("own", 4), ("sibling", 4),
+        ("outer", 0), ("first", 1, 3, True), ("send", 1), ("send", 3), ("send", 2),
+        ("second", 1, 0, 1), ("first", 3, 5, True), ("second", 2, 0, 1), ("pass", 1), ("pass", 3),
+        ("pass", 2), ("second", 1, 1, 5), ("first", 5, 8, True), ("second", 2, 1, 5),
+        ("second", 1, 5, 8), ("features",), ("own", 0), ("sibling", 0), ("own", 1),
+        ("second", 2, 5, 8), ("second", 3, 0, 4), ("sibling", 1), ("own", 2), ("second", 3, 4, 8),
+        ("sibling", 2), ("own", 3), ("sibling", 3), ("opposite",), ("own", 4), ("sibling", 4),
     ),
 )
 

time: 79.9 us -> 79.9 us (level)
  no operation moved by 1% of the time
where the time goes in v6:
time: 79.9 us; the launch traced here: 79.5 us
  Pallas kernels  77.4 us (97%)
  local copies, waits for them, and re-layouts  1.42 us (2%)
    pallas_call x1, Pallas kernels, body(): pl.pallas_call(kernel, out_shape=(jax.ShapeDtypeStruct((1, TOK), F32), ja...  77.4 us

profile of v6, /device:TPU:1, one launch (start us, length us, event | category | flops | bytes accessed | tf_op | source)
XLA Modules:
  0.0 79.5 jit_solution(16431300682899185686)
XLA Ops:
  0.6 77.4 %shard_map.59 = (f32[1,128]{1,0:T(1,128)S(1)}, bf16[128,1344]{1,0:T(8,128)(2,1)S(1)}) custom-call(bf16[1344,128]{1,0:T(8,128)(2,1)} %bitcast.5, bf16[8,5376]{1,0:T(8,128)(2,1)} %emb_hbm.1, s32[1,128]{1,0:T(1,128)} %bitcast.6, f32[1,128]{1,0:T(1,128)} %bitcast.7), custom_call_target="tpu_custom_call" | custom-call | flops 4227858432 | bytes 2752512 | tf_op jit(solution)/shard_map/pallas_call | solution.py:527
  78.0 0.9 %copy.6 = bf16[128,1344]{0,1:T(8,128)(2,1)} copy(bf16[128,1344]{1,0:T(8,128)(2,1)S(1)} %get-tuple-element.7) | data formatting | bytes 688128
  79.0 0.5 copy.8

commit v7 on v6

--- a/solution.py
+++ b/solution.py
@@ -487,10 +487,22 @@
     add_first(5)
     add_last(2)
     add_last(3)
-    multiply(6)
+    @pl.when(c == 0)
+    def _():
+        multiply(6)
+
     add_last(4)
-    multiply(7)
+
+    @pl.when(c == 0)
+    def _():
+        multiply(7)
+
     add_last(5)
+
+    @pl.when(c == 1)
+    def _():
+        multiply(6)
+        multiply(7)
 
     received(lbuf.at[0:NK - 1], l_r.at[0])
     result = jnp.zeros((8, TOK), F32)

time: 79.9 us -> 79.9 us (level)
  no operation moved by 1% of the time
where the time goes in v7:
time: 79.9 us; the launch traced here: 79.8 us
  Pallas kernels  77.7 us (97%)
  local copies, waits for them, and re-layouts  1.42 us (2%)
    pallas_call x1, Pallas kernels, body(): pl.pallas_call(kernel, out_shape=(jax.ShapeDtypeStruct((1, TOK), F32), ja...  77.7 us

profile of v7, /device:TPU:1, one launch (start us, length us, event | category | flops | bytes accessed | tf_op | source)
XLA Modules:
  0.0 79.8 jit_solution(1014629517787487468)
XLA Ops:
  0.6 77.7 %shard_map.59 = (f32[1,128]{1,0:T(1,128)S(1)}, bf16[128,1344]{1,0:T(8,128)(2,1)S(1)}) custom-call(bf16[1344,128]{1,0:T(8,128)(2,1)} %bitcast.5, bf16[8,5376]{1,0:T(8,128)(2,1)} %emb_hbm.1, s32[1,128]{1,0:T(1,128)} %bitcast.6, f32[1,128]{1,0:T(1,128)} %bitcast.7), custom_call_target="tpu_custom_call" | custom-call | flops 4227858432 | bytes 2752512 | tf_op jit(solution)/shard_map/pallas_call | solution.py:539
  78.4 0.9 %copy.6 = bf16[128,1344]{0,1:T(8,128)(2,1)} copy(bf16[128,1344]{1,0:T(8,128)(2,1)S(1)} %get-tuple-element.7) | data formatting | bytes 688128
  79.3 0.5 copy.8
